TPU v7x, 256 devices: a whole 4x4x8 slice. The times are simulated.
256 devices in a mesh: branch: 8 (over x, y_lo), expert: 32 (over z, y_hi, core).
Axes of the slice: x: 4, y: 4 (y_hi: 2, y_lo: 2; y = y_hi * 2 + y_lo), z: 8, core: 2. Of those that a mesh axis runs over, the one named last changes fastest.
Arguments:
- residual: bfloat16 [2048, 4096], P('branch', 'expert'), may hold values from -6 to 6
- heads_out: bfloat16 [2048, 4096], P('branch', 'expert'), may hold values from -6 to 6
- out_proj: bfloat16 [8, 4096, 4096], P('branch', 'expert'), may hold values from -0.25 to 0.25
- norm_gain: bfloat16 [4096], P('expert'), may hold values from 0.5 to 2
- gate_w: bfloat16 [8, 4096, 8192], P('branch', None, 'expert'), may hold values from -0.09375 to 0.09375
- up_w: bfloat16 [8, 4096, 8192], P('branch', None, 'expert'), may hold values from -0.09375 to 0.09375
- down_w: bfloat16 [8, 8192, 4096], P('branch', 'expert'), may hold values from -0.0625 to 0.0625
- expert_ids: int32 [2048, 2], P('branch'), may hold values from 0 to 7, all different within a row; in each aligned block of 256 rows (0 to 255, 256 to 511, ...) at most 96 rows name the same one
- gate_slots: int32 [2048, 2], P('branch'), may hold values from 0 to 63
- gate_table: float32 [64], replicated, may hold values from 0.25 to 4
Outputs:
- layer_out: bfloat16 [2048, 4096], P('branch', 'expert')
Inputs may be any that keep to these rules, and one draw needn't show every extreme that they name: `expert_ids`: each token names two different experts. In each aligned block of 256 tokens no expert is named by more than 96 tokens, a bound that some block reaches.
All inputs are finite; a program needn't handle non-finite values.
Results may differ from a plain program's by a relative error of at most 0.02.
Values may be sent and summed in bfloat16 or wider, within the bound.
A program may use at most 64 MiB of HBM per device.

v0:
```python
import jax
import jax.numpy as jnp
from jax import lax
from jax.sharding import PartitionSpec as P

D = 4096
SLOTS = 64


def per_device(
    residual,
    heads_out,
    out_proj,
    norm_gain,
    gate_w,
    up_w,
    down_w,
    expert_ids,
    gate_slots,
    gate_table,
):
    branches = lax.axis_size("branch")
    tok_rows, d_local = residual.shape
    capacity = 3 * tok_rows // branches
    rows_total = branches * capacity
    local_proj = out_proj[0].astype(jnp.float32)
    summed = lax.psum(local_proj.astype(jnp.bfloat16), "branch").astype(jnp.float32)
    merged = (summed / branches).astype(jnp.bfloat16)
    attn_term = jnp.dot(heads_out, merged, preferred_element_type=jnp.float32)
    attn = lax.psum_scatter(
        attn_term.astype(jnp.bfloat16), "expert", scatter_dimension=1, tiled=True
    ).astype(jnp.float32)
    stream = residual.astype(jnp.float32) + attn
    squares = lax.psum(jnp.sum(stream * stream, axis=1), "expert")
    mean_sq = squares / D
    normed = (
        stream * lax.rsqrt(mean_sq[:, None] + 1e-05) * norm_gain.astype(jnp.float32)[None, :]
    ).astype(jnp.bfloat16)
    flat_ids = expert_ids.reshape(-1)
    onehot = (flat_ids[:, None] == jnp.arange(branches, dtype=jnp.int32)[None, :]).astype(jnp.int32)
    ranks = jnp.cumsum(onehot, axis=0) - 1
    slot = jnp.sum(ranks * onehot, axis=1)
    position = flat_ids * capacity + slot
    selected = position[:, None] == jnp.arange(rows_total, dtype=jnp.int32)[None, :]
    sel_pair = selected.reshape(tok_rows, 2, rows_total)
    dispatch_map = jnp.logical_or(sel_pair[:, 0], sel_pair[:, 1]).astype(jnp.bfloat16)
    buffer = lax.dot_general(
        dispatch_map, normed, (((0,), (0,)), ((), ())), preferred_element_type=jnp.float32
    )
    buffer = buffer.astype(jnp.bfloat16).reshape(branches, capacity, d_local)
    arrived = lax.all_to_all(buffer, "branch", split_axis=0, concat_axis=0, tiled=True)
    gate_local = gate_w[0]
    up_local = up_w[0]
    piece = lax.all_gather(arrived, "expert", axis=2, tiled=True)
    width = piece.shape[2]
    rows = piece.reshape(rows_total, width)
    gate = jnp.dot(rows, gate_local, preferred_element_type=jnp.float32)
    upper = jnp.dot(rows, up_local, preferred_element_type=jnp.float32)
    hidden = (jax.nn.silu(gate) * upper).astype(jnp.bfloat16)
    table_hits = (
        gate_slots[:, :, None] == jnp.arange(SLOTS, dtype=jnp.int32)[None, None, :]
    ).astype(jnp.float32)
    raw_gates = jnp.sum(table_hits * gate_table[None, None, :], axis=2)
    gates = raw_gates / jnp.sum(raw_gates, axis=1, keepdims=True)
    down_local = down_w[0]
    summed_rows = lax.psum_scatter(
        lax.dot_general(
            down_local, hidden, (((0,), (1,)), ((), ())), preferred_element_type=jnp.float32
        ).astype(jnp.bfloat16),
        "expert",
        scatter_dimension=0,
        tiled=True,
    ).astype(jnp.float32)
    returned = lax.all_to_all(
        summed_rows.reshape(d_local, branches, capacity).astype(jnp.bfloat16),
        "branch",
        split_axis=1,
        concat_axis=1,
        tiled=True,
    ).astype(jnp.float32)
    returned = returned.reshape(d_local, rows_total)
    ffn = jnp.zeros((tok_rows, d_local), jnp.float32)
    for choice_index in range(2):
        picked = lax.dot_general(
            sel_pair[:, choice_index].astype(jnp.float32),
            returned,
            (((1,), (1,)), ((), ())),
            precision=lax.Precision.HIGHEST,
            preferred_element_type=jnp.float32,
        )
        ffn = ffn + gates[:, choice_index : choice_index + 1] * picked
    return (stream + ffn).astype(jnp.bfloat16)


def solution(mesh):
    return jax.shard_map(
        per_device,
        mesh=mesh,
        in_specs=(
            P("branch", "expert"),
            P("branch", "expert"),
            P("branch", "expert", None),
            P("expert"),
            P("branch", None, "expert"),
            P("branch", None, "expert"),
            P("branch", "expert", None),
            P("branch", None),
            P("branch", None),
            P(),
        ),
        out_specs=P("branch", "expert"),
        check_vma=False,
    )
```

profile of v0, /device:TPU:1, one launch (start us, length us, event | category | flops | bytes accessed | tf_op | source)
XLA Modules:
  0.0 566.9 jit_solution(11767455778142191193)
XLA Ops:
  6.5 0.0 copy-start
  6.5 0.0 all-reduce.2.cloned.1.call-start
  6.5 0.7 all-reduce.2.cloned.1.call-update
  7.3 0.0 copy-start.3
  7.3 0.0 reduce-scatter.5.cloned.1.call-start
  7.3 85.0 %all-reduce.2.cloned.1.call-done = bf16[128,4096]{1,0:T(8,128)(2,1)} async-done(((bf16[128,4096]{1,0:T(8,128)(2,1)}), bf16[128,4096]{1,0:T(8,128)(2,1)}) %all-reduce.2.cloned.1.call-update) | async-done | bytes 1048592 | tf_op jit(solution)/shard_map/psum | solution.py:27
  92.3 3.3 fusion.1
  95.6 0.0 copy-start.1
  95.6 0.0 copy-start.6
  95.6 0.0 reduce-scatter.5.cloned.1.call-update
  95.6 0.0 all-gather.2.cloned.1.call-start
  95.7 0.0 copy-done.3
  95.7 0.1 copy.48
  95.8 0.1 eq.59
  96.0 0.1 eq.55
  96.2 1.1 reduce-window.6
  97.3 0.2 slice_reduce_fusion
  97.6 0.1 fusion.27
  97.6 0.1 reduce_sum.41
  97.8 0.1 copy.50
  97.9 0.0 copy-done.1
  97.9 0.1 copy.47
  98.0 0.0 copy-done.6
  98.0 0.3 iota_compare_fusion
  98.3 115.9 %reduce-scatter.5.cloned.1.call-done = bf16[256,128]{0,1:T(8,128)(2,1)} async-done(((bf16[256,4096]{0,1:T(8,128)(2,1)}), bf16[256,128]{0,1:T(8,128)(2,1)}) %reduce-scatter.5.cloned.1.call-update) | async-done | bytes 65552 | tf_op jit(solution)/shard_map/reduce_scatter | solution.py:30
  214.2 0.9 multiply_reduce_fusion
  215.1 70.3 %psum.15 = f32[256]{0:T(256)S(1)} all-reduce(f32[256]{0:T(256)S(1)} %multiply_reduce_fusion), channel_id=1, replica_groups=mesh['branch'=8,'expert'=32] {'expert'}, use_global_device_ids=true, to_apply=%region_8.9 | all-reduce | flops 256 | bytes 2048 | tf_op jit(solution)/shard_map/psum | solution.py:34
  285.4 1.3 convolution_convert_fusion.2
  286.7 9.6 %all_to_all.10 = bf16[8,96,128]{2,1,0:T(8,128)(2,1)} all-to-all(bf16[8,96,128]{2,1,0:T(8,128)(2,1)S(1)} %bitcast.53), channel_id=1, replica_groups=mesh['branch'=8,'expert'=32] {'branch'}, dimensions={0} | all-to-all | bytes 393216 | tf_op jit(solution)/shard_map/all_to_all | solution.py:51
  296.3 0.0 all-gather.2.cloned.1.call-update
  296.3 0.0 reduce-scatter.7.cloned.1.call-start
  296.3 95.7 %all-gather.2.cloned.1.call-done = bf16[8,96,4096]{2,1,0:T(8,128)(2,1)} async-done(((bf16[8,96,128]{2,1,0:T(8,128)(2,1)}), bf16[8,96,4096]{2,1,0:T(8,128)(2,1)}) %all-gather.2.cloned.1.call-update) | async-done | bytes 6291472 | tf_op jit(solution)/shard_map/all_gather | solution.py:54
  392.0 5.2 fusion.5
  397.2 0.0 copy-done
  397.2 12.7 %fusion = bf16[4096,768]{0,1:T(8,128)(2,1)} fusion(bf16[1,256,4096]{2,1,0:T(8,128)(2,1)S(1)} %copy-done, bf16[768,4096]{1,0:T(8,128)(2,1)} %bitcast.57, bf16[1,4096,256]{2,1,0:T(8,128)(2,1)} %param.15, f32[768,256]{1,0:T(8,128)S(1)} %fusion.5), kind=kOutput, calls=%fused_computation.1 | convolution fusion | flops 3225550848 | bytes 17563648 | tf_op jit(solution)/shard_map/dot_general | solution.py:67
  409.9 8.7 %copy.56 = bf16[4096,768]{1,0:T(8,128)(2,1)} copy(bf16[4096,768]{0,1:T(8,128)(2,1)} %fusion) | data formatting | bytes 12582912
  418.6 0.0 reduce-scatter.7.cloned.1.call-update
  418.6 0.7 copy-done.4
  419.2 0.0 copy-done.5
  419.2 0.1 select_reduce_fusion
  419.4 128.3 %reduce-scatter.7.cloned.1.call-done = bf16[128,768]{1,0:T(8,128)(2,1)} async-done(((bf16[4096,768]{1,0:T(8,128)(2,1)}), bf16[128,768]{1,0:T(8,128)(2,1)}) %reduce-scatter.7.cloned.1.call-update) | async-done | bytes 196624
  547.7 1.7 copy.57
  549.4 4.0 all-to-all-start.1
  553.5 5.5 all-to-all-done.1
  559.0 0.3 convolution_multiply_fusion.1
  559.3 0.0 copy-done.2
  559.3 0.3 fusion.17
  559.6 0.7 copy.53
  (11 shorter events, 0.1 us)
Async XLA Ops:
  6.5 390.7 %copy-start = (bf16[1,256,4096]{2,1,0:T(8,128)(2,1)S(1)}, bf16[1,256,4096]{2,1,0:T(8,128)(2,1)}, u32[]{:S(2)}) copy-start(bf16[1,256,4096]{2,1,0:T(8,128)(2,1)} %param.16) | copy-start | bytes 6291460
  6.5 85.7 %all-reduce.2.cloned.1.call-start = ((), (), s32[]{:S(2)}) async-start(), calls=%async_computation.4 | async-start | bytes 2097152 | tf_op jit(solution)/shard_map/psum | solution.py:27
  7.3 88.4 %copy-start.3 = (s32[256,2]{0,1:T(2,128)S(1)}, s32[256,2]{0,1:T(2,128)}, u32[]{:S(2)}) copy-start(s32[256,2]{0,1:T(2,128)} %param.17) | copy-start | bytes 6148
  7.3 206.9 %reduce-scatter.5.cloned.1.call-start = ((), (), s32[]{:S(2)}) async-start(), calls=%async_computation.5 | async-start | bytes 2162688 | tf_op jit(solution)/shard_map/reduce_scatter | solution.py:30
  95.6 2.3 copy-start.1
  95.6 2.4 copy-start.6
  95.6 296.4 %all-gather.2.cloned.1.call-start = ((), (), s32[]{:S(2)}) async-start(), calls=%async_computation.6 | async-start | bytes 6488064 | tf_op jit(solution)/shard_map/all_gather | solution.py:54
  296.3 251.4 %reduce-scatter.7.cloned.1.call-start = ((), (), s32[]{:S(2)}) async-start(), calls=%async_computation.7 | async-start | bytes 6488064
  418.6 0.7 copy-start.4
  418.6 0.7 copy-start.5
  418.6 140.7 %copy-start.2 = (bf16[256,128]{0,1:T(8,128)(2,1)S(1)}, bf16[256,128]{0,1:T(8,128)(2,1)}, u32[]{:S(2)}) copy-start(bf16[256,128]{0,1:T(8,128)(2,1)} %reduce-scatter.5.cloned.1.call-done) | copy-start | bytes 196612
  549.4 9.5 %all-to-all-start.1 = ((bf16[128,8,96]{0,2,1:T(8,128)(2,1)}), bf16[128,8,96]{0,2,1:T(8,128)(2,1)S(1)}, u32[]{:S(2)}, u32[]{:S(2)}) async-start(bf16[128,8,96]{0,2,1:T(8,128)(2,1)} %bitcast.13), calls=%async_computation.2 | async-start | bytes 393216 | tf_op jit(solution)/shard_map/all_to_all | solution.py:74
Sparse Core Ops, SparseCore 0:
  10.0 82.2 all-reduce.1
  96.4 117.7 reduce-scatter.4
  296.4 95.5 all-gather.1
  418.7 128.9 reduce-scatter.6
where the time goes:
time: 572 us; the launch traced here: 567 us
  waiting for transfers between devices  431 us (75%)
  blocking collectives  79.8 us (14%)
  matrix products  23.2 us (4%)
  between operations  13.3 us (2%)
  local copies, waits for them, and re-layouts  12.8 us (2%)
    unnamed x5, waiting for transfers between devices  129 us
    reduce_scatter x1, waiting for transfers between devices, per_device(): lax.psum_scatter(attn_term.astype(jnp.bfloat16), 'expert', scatter_dimens...  116 us
    all_gather x1, waiting for transfers between devices, per_device(): piece = lax.all_gather(arrived, 'expert', axis=2, tiled=True)  95.7 us
    psum x1, waiting for transfers between devices, per_device(): lax.psum(local_proj.astype(jnp.bfloat16), 'branch').astype(jnp.float32)  85 us
    psum x1, blocking collectives, per_device(): squares = lax.psum(jnp.sum(stream * stream, axis=1), 'expert')  70.3 us
    dot_general x1, matrix products, per_device(): lax.dot_general(down_local, hidden, (((0,), (1,)), ((), ())), preferred_e...  12.7 us
  transfers between devices with their start and end apart: 5, of which 5 were waited for; matrix products, arithmetic and copies ran while one was open for 0% of the time, Pallas kernels for 0%

commit v1 on v0

v1 whole, which is shorter than its diff:
```python
import jax
import jax.numpy as jnp
from jax import lax
from jax.experimental import pallas as pl
from jax.experimental.pallas import tpu as pltpu
from jax.sharding import PartitionSpec as P

MESH = pl.DeviceIdType.MESH
F32, BF16 = jnp.float32, jnp.bfloat16
D = 4096
SLOTS = 64
NB = 8
NZ = 8
TOK = 256
CAP = 96
ROWS = 4 * CAP
GROWS = 16
BLK = ROWS + GROWS
FW = 128
CW = 256
HALF_A = 208
HALF_E = ROWS // 2


def rcopy(src, dst, send_sem, recv_sem, dev):
    return pltpu.make_async_remote_copy(
        src_ref=src, dst_ref=dst, send_sem=send_sem, recv_sem=recv_sem,
        device_id=dev, device_id_type=MESH)


def kernel(res_hbm, heads_hbm, op_hbm, gain_ref, gate_hbm, up_hbm, down_hbm, idst_ref, slots_ref,
           table_ref, out_ref,
           res_v, heads_v, op_in, merged, w4, dn, s0, s1, b_snd, b_rcv, tot, y_snd, y_rcv, t_snd, t_rcv,
           stream, dsp, xg, acc, sq, hid, e_part, e_snd, e_rcv, e_keep, ey_snd, ey_rcv, ret_snd, ret_v,
           loc, w_s, w_r, h_s, h_r, hf_s, hf_r, op_s, op_r, b_s, b_r, yt_s, yt_r, g_s, g_r,
           c_s, c_r, ag_s, ag_r, agy_s, agy_r, e_s, e_r, ey_s, ey_r, f_s, f_r):
    b = lax.axis_index("branch")
    e = lax.axis_index("expert")
    z = e // 4
    yh = (e // 2) % 2
    c = e % 2
    half = b // 4
    sib = (b, e + 1 - 2 * c)
    right = (b, ((z + 1) % NZ) * 4 + yh * 2 + c)
    left = (b, ((z + NZ - 1) % NZ) * 4 + yh * 2 + c)
    ypart = (b, z * 4 + (1 - yh) * 2 + c)
    tpart = (z, b * 4 + c * 2 + yh)
    t_self = jnp.logical_and(z == b, yh == c)
    dirs = (right, left)

    def chip_dev(j, core):
        return (j, z * 4 + yh * 2 + core)

    loads = [
        pltpu.make_async_copy(res_hbm, res_v, loc.at[0]),
        pltpu.make_async_copy(
            heads_hbm,
            heads_v.at[pl.ds(pl.multiple_of(b * TOK, TOK), TOK), pl.ds(pl.multiple_of(c * FW, FW), FW)],
            loc.at[1]),
        pltpu.make_async_copy(
            op_hbm.at[:, pl.ds(pl.multiple_of((b * 2 + c) * CW, CW), CW)], op_in.at[b * 2 + c], loc.at[2]),
        pltpu.make_async_copy(gate_hbm, w4.at[0], loc.at[3]),
        pltpu.make_async_copy(up_hbm, w4.at[2], loc.at[4]),
        pltpu.make_async_copy(down_hbm, dn.at[0], loc.at[5]),
    ]
    for ld in loads:
        ld.start()

    barrier = pltpu.get_barrier_semaphore()
    for kb in range(NB):
        for kc in range(2):
            if kb or kc:
                pl.semaphore_signal(barrier, inc=1, device_id=chip_dev((b + kb) % NB, (c + kc) % 2),
                                    device_id_type=MESH)
    for dev in (right, left, ypart):
        pl.semaphore_signal(barrier, inc=1, device_id=dev, device_id_type=MESH)

    @pl.when(jnp.logical_not(t_self))
    def _():
        pl.semaphore_signal(barrier, inc=1, device_id=tpart, device_id_type=MESH)

    pl.semaphore_wait(barrier, jnp.where(t_self, 18, 19))

    pend = []
    my_heads = heads_v.at[pl.ds(pl.multiple_of(b * TOK, TOK), TOK), pl.ds(pl.multiple_of(c * FW, FW), FW)]
    for k in range(1, NB):
        cp = rcopy(heads_hbm, my_heads, h_s.at[k - 1], h_r.at[k - 1], chip_dev((b + k) % NB, c))
        cp.start()
        pend.append(cp)
    for kb in range(NB):
        for kc in range(2):
            if kb or kc:
                j, cc = (b + kb) % NB, (c + kc) % 2
                cp = rcopy(op_hbm.at[:, pl.ds(pl.multiple_of((j * 2 + cc) * CW, CW), CW)],
                           op_in.at[b * 2 + c], op_s.at[kb * 2 + kc], op_r.at[kb * 2 + kc], chip_dev(j, cc))
                cp.start()
                pend.append(cp)
    for i, (src, dst) in enumerate(((gate_hbm, w4.at[1]), (up_hbm, w4.at[3]), (down_hbm, dn.at[1]))):
        cp = rcopy(src, dst, w_s.at[i], w_r.at[i], sib)
        cp.start()
        pend.append(cp)

    me = z * 2 + yh
    gain_at = (me, pl.ds(ROWS, GROWS), pl.ds(pl.multiple_of(c * FW, FW), FW))
    xg[gain_at] = jnp.broadcast_to(gain_ref[...], (GROWS, FW))
    gain_cp = rcopy(xg.at[gain_at], xg.at[gain_at], g_s, g_r, sib)
    gain_cp.start()
    pend.append(gain_cp)

    ids = idst_ref[...]
    xi = lax.broadcasted_iota(jnp.int32, (16, TOK), 0)
    named = ((ids[0:1] == xi) | (ids[1:2] == xi)).astype(BF16)
    before = (lax.broadcasted_iota(jnp.int32, (TOK, TOK), 0)
              < lax.broadcasted_iota(jnp.int32, (TOK, TOK), 1)).astype(BF16)
    rank = jnp.dot(named, before, preferred_element_type=F32).astype(jnp.int32)
    ci = lax.broadcasted_iota(jnp.int32, (CAP, TOK), 0)
    for x in range(NB):
        hit = rank[x:x + 1] == ci
        s0[x * CAP:(x + 1) * CAP] = (hit & (ids[0:1] == x)).astype(BF16)
        s1[x * CAP:(x + 1) * CAP] = (hit & (ids[1:2] == x)).astype(BF16)
    acc[...] = jnp.zeros_like(acc)
    sq[...] = jnp.zeros_like(sq)

    loads[1].wait()
    for k in range(1, NB):
        src_b = (b + NB - k) % NB
        rcopy(heads_hbm,
              heads_v.at[pl.ds(pl.multiple_of(src_b * TOK, TOK), TOK), pl.ds(pl.multiple_of(c * FW, FW), FW)],
              h_s.at[k - 1], h_r.at[k - 1], sib).wait_recv()
    mine_cols = heads_v.at[:, pl.ds(pl.multiple_of(c * FW, FW), FW)]
    their_cols = heads_v.at[:, pl.ds(pl.multiple_of((1 - c) * FW, FW), FW)]
    cp = rcopy(mine_cols, mine_cols, hf_s, hf_r, sib)
    cp.start()
    pend.append(cp)

    loads[2].wait()
    for kb in range(NB):
        for kc in range(2):
            if kb or kc:
                rcopy(op_hbm.at[:, pl.ds(0, CW)], op_in.at[((b + NB - kb) % NB) * 2 + (c + kc) % 2],
                      op_s.at[kb * 2 + kc], op_r.at[kb * 2 + kc], sib).wait_recv()
    for cc in range(2):
        total = op_in[cc].astype(F32)
        for j in range(1, NB):
            total = total + op_in[j * 2 + cc].astype(F32)
        merged[cc * FW:(cc + 1) * FW] = (total / NB).astype(BF16)
    rcopy(their_cols, their_cols, hf_s, hf_r, sib).wait_recv()

    def attn_part(zd):
        return jnp.dot(heads_v[pl.ds(pl.multiple_of(zd * TOK, TOK), TOK), :], merged[...],
                       preferred_element_type=F32)

    def b_copy(d, s):
        if s == 0:
            rows = pl.ds(d * 128, 128)
            return rcopy(b_snd.at[d, 0, rows], b_rcv.at[d, 0, rows], b_s.at[d, s], b_r.at[d, s], dirs[d])
        return rcopy(b_snd.at[d, s], b_rcv.at[d, s], b_s.at[d, s], b_r.at[d, s], dirs[d])

    p = attn_part((z + 4) % NZ)
    b_snd[0, 0, 0:128] = p[0:128].astype(BF16)
    b_snd[1, 0, 128:256] = p[128:256].astype(BF16)
    for d in range(2):
        b_copy(d, 0).start()
    for s in range(1, 4):
        for d in range(2):
            zd = (z + (4 - s)) % NZ if d == 0 else (z + NZ - (4 - s)) % NZ
            tot[d] = attn_part(zd)
        for d in range(2):
            b_copy(d, s - 1).wait_recv()
            if s == 1:
                lo, hi = (0, 128) if d == 0 else (128, 256)
                b_snd[d, s, lo:hi] = (tot[d, lo:hi] + b_rcv[d, 0, lo:hi].astype(F32)).astype(BF16)
                b_snd[d, s, 128 - lo:384 - hi] = tot[d, 128 - lo:384 - hi].astype(BF16)
            else:
                b_snd[d, s] = (tot[d] + b_rcv[d, s - 1].astype(F32)).astype(BF16)
            b_copy(d, s).start()
    tot[0] = attn_part(z)
    for d in range(2):
        b_copy(d, 3).wait_recv()
    tot[0] = tot[0] + b_rcv[0, 3].astype(F32) + b_rcv[1, 3].astype(F32)
    for d in range(2):
        for s in range(4):
            pend.append(b_copy(d, s))
    y_snd[...] = tot[0, :, pl.ds(pl.multiple_of((1 - yh) * FW, FW), FW)].astype(BF16)
    cp = rcopy(y_snd, y_rcv, yt_s.at[0], yt_r.at[0], ypart)
    cp.start()
    pend.append(cp)
    cp.wait_recv()
    t_snd[...] = (tot[0, :, pl.ds(pl.multiple_of(yh * FW, FW), FW)] + y_rcv[...].astype(F32)).astype(BF16)
    t_copy = rcopy(t_snd, t_rcv, yt_s.at[1], yt_r.at[1], tpart)

    @pl.when(t_self)
    def _():
        t_rcv[...] = t_snd[...]

    @pl.when(jnp.logical_not(t_self))
    def _():
        t_copy.start()
        t_copy.wait_recv()

    loads[0].wait()
    st = res_v[...].astype(F32) + t_rcv[...].astype(F32)
    stream[...] = st
    scaled = (st * gain_ref[...].astype(F32)).astype(BF16)
    dsp[...] = jnp.dot(s0[...] + s1[...], scaled, preferred_element_type=F32).astype(BF16)
    blk_at = (me, pl.ds(pl.multiple_of((b % 4) * CAP, CAP), CAP), pl.ds(pl.multiple_of(c * FW, FW), FW))
    my_src = half == c

    def c_copy(k):
        x = (b + k) % NB
        return rcopy(dsp.at[pl.ds(pl.multiple_of(x * CAP, CAP), CAP)], xg.at[blk_at], c_s.at[k],
                     c_r.at[(b % 4) * 2 + c], chip_dev(x, half))

    own_blk = pltpu.make_async_copy(dsp.at[pl.ds(pl.multiple_of(b * CAP, CAP), CAP)], xg.at[blk_at], loc.at[6])
    for k in range(1, NB):
        c_copy(k).start()
        pend.append(c_copy(k))

    @pl.when(my_src)
    def _():
        own_blk.start()

    @pl.when(jnp.logical_not(my_src))
    def _():
        c_copy(0).start()

    for i in range(8):
        @pl.when(jnp.logical_not(jnp.logical_and(my_src, (b % 4) * 2 + c == i)))
        def _(i=i):
            rcopy(dsp.at[pl.ds(0, CAP)], xg.at[me, pl.ds((i // 2) * CAP, CAP), pl.ds((i % 2) * FW, FW)],
                  c_s.at[0], c_r.at[i], sib).wait_recv()

    @pl.when(my_src)
    def _():
        own_blk.wait()

    sib_gain = xg.at[me, pl.ds(ROWS, GROWS), pl.ds(pl.multiple_of((1 - c) * FW, FW), FW)]
    rcopy(sib_gain, sib_gain, g_s, g_r, sib).wait_recv()

    def ag_copy(d, t, s, slot):
        if s == 3:
            ref = xg.at[slot, pl.ds(0, HALF_A)] if d == 0 else xg.at[slot, pl.ds(HALF_A, BLK - HALF_A)]
        else:
            ref = xg.at[slot]
        return rcopy(ref, ref, ag_s.at[d, t, s], ag_r.at[d, t, s], dirs[d])

    def gate_up(slot):
        blk = xg[slot, 0:ROWS]
        inv = 1.0 / xg[slot, ROWS:BLK][0:1].astype(F32)
        v = blk.astype(F32) * inv
        sq[...] += v * v
        rows = pl.ds(pl.multiple_of(slot * CW, CW), CW)

        def part(i, carry):
            acc[i] += jnp.dot(xg[slot, 0:ROWS], w4[i, rows, :], preferred_element_type=F32)
            return carry
        lax.fori_loop(0, 4, part, 0)

    def start(cp):
        cp.start()
        pend.append(cp)

    other = z * 2 + 1 - yh
    start(rcopy(xg.at[me], xg.at[me], agy_s, agy_r, ypart))
    for d in range(2):
        start(ag_copy(d, 0, 0, me))
    loads[3].wait()
    loads[4].wait()
    for i in range(2):
        rcopy(gate_hbm, w4.at[1 + 2 * i], w_s.at[i], w_r.at[i], sib).wait_recv()
    gate_up(me)
    rcopy(xg.at[other], xg.at[other], agy_s, agy_r, ypart).wait_recv()
    for d in range(2):
        start(ag_copy(d, 1, 0, other))
    gate_up(other)
    for s in range(1, 4):
        for t in range(2):
            yy = yh if t == 0 else 1 - yh
            slots = [((z + NZ - s) % NZ) * 2 + yy, ((z + s) % NZ) * 2 + yy]
            for d in range(2):
                ag_copy(d, t, s - 1, slots[d]).wait_recv()
                start(ag_copy(d, t, s, slots[d]))
            for d in range(2):
                gate_up(slots[d])
    for t in range(2):
        yy = yh if t == 0 else 1 - yh
        slot = ((z + 4) % NZ) * 2 + yy
        for d in range(2):
            ag_copy(d, t, 3, slot).wait_recv()
        gate_up(slot)

    scale = lax.rsqrt(jnp.sum(sq[...], axis=1, keepdims=True) / D + 1e-05)
    for i in range(2):
        g = acc[i] * scale
        hid[i] = (g / (1.0 + jnp.exp(-g)) * (acc[2 + i] * scale)).astype(BF16)
    loads[5].wait()
    rcopy(down_hbm, dn.at[1], w_s.at[2], w_r.at[2], sib).wait_recv()

    def down_part(zd, t):
        yy = 1 - yh if t == 0 else yh
        cols = pl.ds(pl.multiple_of((zd * 2 + yy) * CW, CW), CW)
        return (jnp.dot(hid[0], dn[0, :, cols], preferred_element_type=F32)
                + jnp.dot(hid[1], dn[1, :, cols], preferred_element_type=F32))

    def e_copy(d, t, s):
        if s == 0:
            rows = pl.ds(d * HALF_E, HALF_E)
            return rcopy(e_snd.at[d, t, 0, rows], e_rcv.at[d, t, 0, rows], e_s.at[d, t, s], e_r.at[d, t, s],
                         dirs[d])
        return rcopy(e_snd.at[d, t, s], e_rcv.at[d, t, s], e_s.at[d, t, s], e_r.at[d, t, s], dirs[d])

    for t in range(2):
        p = down_part((z + 4) % NZ, t)
        e_snd[0, t, 0, 0:HALF_E] = p[0:HALF_E].astype(BF16)
        e_snd[1, t, 0, HALF_E:ROWS] = p[HALF_E:ROWS].astype(BF16)
        for d in range(2):
            start(e_copy(d, t, 0))
    for s in range(1, 4):
        for t in range(2):
            for d in range(2):
                e_part[d, t] = down_part((z + (4 - s)) % NZ if d == 0 else (z + NZ - (4 - s)) % NZ, t)
        for t in range(2):
            for d in range(2):
                e_copy(d, t, s - 1).wait_recv()
                if s == 1:
                    lo, hi = (0, HALF_E) if d == 0 else (HALF_E, ROWS)
                    e_snd[d, t, s, lo:hi] = (e_part[d, t, lo:hi] + e_rcv[d, t, 0, lo:hi].astype(F32)).astype(BF16)
                    lo, hi = HALF_E - lo, ROWS + HALF_E - hi
                    e_snd[d, t, s, lo:hi] = e_part[d, t, lo:hi].astype(BF16)
                else:
                    e_snd[d, t, s] = (e_part[d, t] + e_rcv[d, t, s - 1].astype(F32)).astype(BF16)
                start(e_copy(d, t, s))
    for t in range(2):
        e_part[0, t] = down_part(z, t)
    for t in range(2):
        for d in range(2):
            e_copy(d, t, 3).wait_recv()
        tail = e_part[0, t] + e_rcv[0, t, 3].astype(F32) + e_rcv[1, t, 3].astype(F32)
        if t == 0:
            ey_snd[...] = tail.astype(BF16)
            ey = rcopy(ey_snd, ey_rcv, ey_s, ey_r, ypart)
            start(ey)
        else:
            e_keep[...] = tail
    ey.wait_recv()
    ret_snd[...] = (e_keep[...] + ey_rcv[...].astype(F32)).astype(BF16)

    def f_copy(i, cc):
        return rcopy(ret_snd.at[pl.ds(i * CAP, CAP), pl.ds(cc * FW, FW)],
                     ret_v.at[pl.ds(pl.multiple_of(b * CAP, CAP), CAP)],
                     f_s.at[i * 2 + cc], f_r.at[b], chip_dev(4 * c + i, cc))

    for i in range(4):
        for cc in range(2):
            to_self = jnp.logical_and(4 * c + i == b, cc == c)
            mine = pltpu.make_async_copy(ret_snd.at[pl.ds(i * CAP, CAP), pl.ds(cc * FW, FW)],
                                         ret_v.at[pl.ds(pl.multiple_of(b * CAP, CAP), CAP)], loc.at[7])

            @pl.when(to_self)
            def _(mine=mine):
                mine.start()
                mine.wait()

            @pl.when(jnp.logical_not(to_self))
            def _(i=i, cc=cc):
                f_copy(i, cc).start()

    slot_i = lax.broadcasted_iota(jnp.int32, (TOK, SLOTS), 1)
    raw = [jnp.sum(jnp.where(slots_ref[:, k:k + 1] == slot_i, table_ref[...], 0.0), axis=1, keepdims=True)
           for k in range(2)]
    norm = raw[0] + raw[1]

    for x in range(NB):
        @pl.when(jnp.logical_not(jnp.logical_and(my_src, b == x)))
        def _(x=x):
            rcopy(ret_snd.at[pl.ds(0, CAP), pl.ds(0, FW)], ret_v.at[pl.ds(x * CAP, CAP)], f_s.at[0], f_r.at[x],
                  sib).wait_recv()
    result = stream[...]
    for k, sel in enumerate((s0, s1)):
        picked = lax.dot_general(sel[...], ret_v[...], (((0,), (0,)), ((), ())), preferred_element_type=F32)
        result = result + raw[k] / norm * picked
    out_ref[...] = result.astype(BF16)

    for cp in pend:
        cp.wait_send()

    @pl.when(jnp.logical_not(t_self))
    def _():
        t_copy.wait_send()

    @pl.when(jnp.logical_not(my_src))
    def _():
        c_copy(0).wait_send()

    for i in range(4):
        for cc in range(2):
            @pl.when(jnp.logical_not(jnp.logical_and(4 * c + i == b, cc == c)))
            def _(i=i, cc=cc):
                f_copy(i, cc).wait_send()


def per_device(residual, heads_out, out_proj, norm_gain, gate_w, up_w, down_w, expert_ids, gate_slots, gate_table):
    any_, vmem = pl.BlockSpec(memory_space=pl.ANY), pl.BlockSpec(memory_space=pltpu.VMEM)
    dma, v = pltpu.SemaphoreType.DMA, pltpu.VMEM
    return pl.pallas_call(
        kernel,
        out_shape=jax.ShapeDtypeStruct((TOK, FW), BF16),
        in_specs=[any_, any_, any_, vmem, any_, any_, any_, vmem, vmem, vmem],
        out_specs=vmem,
        scratch_shapes=[
            v((TOK, FW), BF16), v((NB * TOK, CW), BF16), v((16, FW, CW), BF16), v((CW, CW), BF16),
            v((4, D, CW), BF16), v((2, CW, D), BF16), v((NB * CAP, TOK), BF16), v((NB * CAP, TOK), BF16),
            v((2, 4, TOK, CW), BF16), v((2, 4, TOK, CW), BF16), v((2, TOK, CW), F32),
            v((TOK, FW), BF16), v((TOK, FW), BF16), v((TOK, FW), BF16), v((TOK, FW), BF16),
            v((TOK, FW), F32), v((NB * CAP, FW), BF16), v((16, BLK, CW), BF16), v((4, ROWS, CW), F32),
            v((ROWS, CW), F32), v((2, ROWS, CW), BF16), v((2, 2, ROWS, CW), F32),
            v((2, 2, 4, ROWS, CW), BF16), v((2, 2, 4, ROWS, CW), BF16), v((ROWS, CW), F32),
            v((ROWS, CW), BF16), v((ROWS, CW), BF16), v((ROWS, CW), BF16), v((NB * CAP, FW), BF16),
            dma((8,)), dma((3,)), dma((3,)), dma((7,)), dma((7,)), dma, dma, dma((16,)), dma((16,)),
            dma((2, 4)), dma((2, 4)), dma((2,)), dma((2,)), dma, dma,
            dma((8,)), dma((8,)), dma((2, 2, 4)), dma((2, 2, 4)), dma, dma,
            dma((2, 2, 4)), dma((2, 2, 4)), dma, dma, dma((8,)), dma((8,)),
        ],
        compiler_params=pltpu.CompilerParams(
            collective_id=0, has_side_effects=True, vmem_limit_bytes=60 * 1024 * 1024),
        name="merge_moe",
    )(residual, heads_out, out_proj[0], norm_gain.reshape(1, FW), gate_w[0], up_w[0], down_w[0],
      expert_ids.T, gate_slots, gate_table.reshape(1, SLOTS))


def solution(mesh):
    return jax.shard_map(
        per_device,
        mesh=mesh,
        in_specs=(
            P("branch", "expert"), P("branch", "expert"), P("branch", "expert", None), P("expert"),
            P("branch", None, "expert"), P("branch", None, "expert"), P("branch", "expert", None),
            P("branch", None), P("branch", None), P(),
        ),
        out_specs=P("branch", "expert"),
        check_vma=False,
    )
```

time: 572 us -> 148 us (0.26)
  waiting for transfers between devices: 431 us -> 0 us
  Pallas kernels: 0 us -> 145 us
  blocking collectives: 79.8 us -> 0 us
  matrix products: 23.2 us -> 0 us
  between operations: 13.3 us -> 0.01 us
  local copies, waits for them, and re-layouts: 12.8 us -> 2.93 us
    pallas_call x0 -> x1, Pallas kernels: none -> 145 us  [per_device(): pl.pallas_call(kernel, out_shape=jax.ShapeDtypeStruct((TOK, FW), BF16), i...]
    unnamed x5 -> x0, waiting for transfers between devices: 129 us -> none
    reduce_scatter x1 -> x0, waiting for transfers between devices: 116 us -> none  [per_device(): lax.psum_scatter(attn_term.astype(jnp.bfloat16), 'expert', scatter_dimens...]
    all_gather x1 -> x0, waiting for transfers between devices: 95.7 us -> none  [per_device(): piece = lax.all_gather(arrived, 'expert', axis=2, tiled=True)]
    psum x1 -> x0, waiting for transfers between devices: 85 us -> none  [per_device(): lax.psum(local_proj.astype(jnp.bfloat16), 'branch').astype(jnp.float32)]
    psum x1 -> x0, blocking collectives: 70.3 us -> none  [per_device(): squares = lax.psum(jnp.sum(stream * stream, axis=1), 'expert')]
    dot_general x6 -> x0, matrix products: 23.2 us -> none  [the longest x1 12.7 us: per_device(): lax.dot_general(down_local, hidden, (((0,), (1,)), ((), ())), preferred_e...]
    all_to_all x1 -> x0, blocking collectives: 9.56 us -> none  [per_device(): lax.all_to_all(buffer, 'branch', split_axis=0, concat_axis=0, tiled=True)]
  transfers between devices with their start and end apart: 5 -> 0, of which waited for: 5 -> 0; matrix products, arithmetic and copies ran while one was open for 0% -> 0% of each run, Pallas kernels for 0% -> 0%
where the time goes in v1:
time: 148 us
  Pallas kernels  145 us (98%)
  local copies, waits for them, and re-layouts  2.93 us (2%)
    pallas_call x1, Pallas kernels, per_device(): pl.pallas_call(kernel, out_shape=jax.ShapeDtypeStruct((TOK, FW), BF16), i...  145 us

profile of v1, /device:TPU:1, one launch (start us, length us, event | category | flops | bytes accessed | tf_op | source)
XLA Modules:
  0.0 147.9 jit_solution(6056462751875598330)
XLA Ops:
  0.0 1.5 copy.11.slots_ref
  1.5 145.0 %merge_moe.1 = bf16[256,128]{1,0:T(8,128)(2,1)} custom-call(bf16[256,128]{1,0:T(8,128)(2,1)} %res_hbm.1, bf16[256,128]{1,0:T(8,128)(2,1)} %heads_hbm.1, bf16[128,4096]{1,0:T(8,128)(2,1)} %bitcast.10, bf16[1,128]{1,0:T(2,128)(2,1)} %bitcast.12, bf16[4096,256]{1,0:T(8,128)(2,1)} %bitcast.7, bf16[4096,256]{1,0:T(8,128)(2,1)} %bitcast.8, ...), custom_call_target="tpu_custom_call" | custom-call | tf_op jit(solution)/shard_map/merge_moe/pallas_call | solution.py:405
  146.5 1.5 copy.13

commit v2 on v1

v2 whole, which is shorter than its diff:
```python
import jax
import jax.numpy as jnp
from jax import lax
from jax.experimental import pallas as pl
from jax.experimental.pallas import tpu as pltpu
from jax.sharding import PartitionSpec as P

MESH = pl.DeviceIdType.MESH
F32, BF16 = jnp.float32, jnp.bfloat16
D = 4096
SLOTS = 64
NB = 8
NZ = 8
TOK = 256
CAP = 96
ROWS = 4 * CAP
GROWS = 16
BLK = ROWS + GROWS
FW = 128
CW = 256
RD = 176
RE = 160
HALF_1, HALF_2 = RE // 2, (ROWS - RE) // 2


def rcopy(src, dst, send_sem, recv_sem, dev):
    return pltpu.make_async_remote_copy(
        src_ref=src, dst_ref=dst, send_sem=send_sem, recv_sem=recv_sem,
        device_id=dev, device_id_type=MESH)


def kernel(res_hbm, heads_hbm, op_hbm, gain_ref, gate_hbm, up_hbm, down_hbm, idst_ref, slots_ref,
           table_ref, out_ref,
           res_v, heads_v, op_in, merged, w4, dn, sel, gsum, g_hi, g_lo, b_snd, b_rcv, b_tot, y_snd, y_rcv,
           t_snd, t_rcv, stream, dsp, xg, acc, sq, hid, e0, e1, e0_snd, e0_rcv, e1_snd, e1_rcv, ey_snd, ey_rcv,
           ez_snd, ez_rcv, ret_snd, ret_v,
           loc, w_s, w_r, h_s, h_r, hf_s, hf_r, op_s, op_r, b_s, b_r, yt_s, yt_r, g_s, g_r,
           c_s, c_r, ag_s, ag_r, agy_s, agy_r, e_s, e_r, ex_s, ex_r, ey_s, ey_r, f_s, f_r):
    b = lax.axis_index("branch")
    e = lax.axis_index("expert")
    z = e // 4
    yh = (e // 2) % 2
    c = e % 2
    half = b // 4
    sib = (b, e + 1 - 2 * c)
    right = (b, ((z + 1) % NZ) * 4 + yh * 2 + c)
    left = (b, ((z + NZ - 1) % NZ) * 4 + yh * 2 + c)
    ypart = (b, z * 4 + (1 - yh) * 2 + c)
    grp = (z + b) % NB
    tpart = (grp, b * 4 + c * 2 + yh)
    tsrc = (z, ((b + NZ - z) % NZ) * 4 + c * 2 + yh)
    t_self = (b == 0) & (z == 0) & (yh == c)
    dirs = (right, left)

    def chip_dev(j, core):
        return (j, z * 4 + yh * 2 + core)

    def op_cols(j, core, t):
        first = (j * 2 + core) * CW + (1 - yh if t == 0 else yh) * FW
        return pl.ds(pl.multiple_of(first, FW), FW)

    loads = [
        pltpu.make_async_copy(res_hbm, res_v, loc.at[0]),
        pltpu.make_async_copy(
            heads_hbm,
            heads_v.at[pl.ds(pl.multiple_of(b * TOK, TOK), TOK), pl.ds(pl.multiple_of(c * FW, FW), FW)],
            loc.at[1]),
        pltpu.make_async_copy(op_hbm.at[:, op_cols(b, c, 0)], op_in.at[0, b * 2 + c], loc.at[2]),
        pltpu.make_async_copy(op_hbm.at[:, op_cols(b, c, 1)], op_in.at[1, b * 2 + c], loc.at[8]),
        pltpu.make_async_copy(gate_hbm, w4.at[0], loc.at[3]),
        pltpu.make_async_copy(up_hbm, w4.at[2], loc.at[4]),
        pltpu.make_async_copy(down_hbm, dn.at[0], loc.at[5]),
    ]
    for ld in loads:
        ld.start()

    barrier = pltpu.get_barrier_semaphore()
    for kb in range(NB):
        for kc in range(2):
            if kb or kc:
                pl.semaphore_signal(barrier, inc=1, device_id=chip_dev((b + kb) % NB, (c + kc) % 2),
                                    device_id_type=MESH)
    for dev in (right, left, ypart):
        pl.semaphore_signal(barrier, inc=1, device_id=dev, device_id_type=MESH)

    @pl.when(jnp.logical_not(t_self))
    def _():
        pl.semaphore_signal(barrier, inc=1, device_id=tsrc, device_id_type=MESH)

    pl.semaphore_wait(barrier, jnp.where(t_self, 18, 19))

    pend = []
    my_heads = heads_v.at[pl.ds(pl.multiple_of(b * TOK, TOK), TOK), pl.ds(pl.multiple_of(c * FW, FW), FW)]
    for k in range(1, NB):
        cp = rcopy(heads_hbm, my_heads, h_s.at[k - 1], h_r.at[k - 1], chip_dev((b + k) % NB, c))
        cp.start()
        pend.append(cp)
    for t in range(2):
        for kb in range(NB):
            for kc in range(2):
                if kb or kc:
                    j, cc = (b + kb) % NB, (c + kc) % 2
                    cp = rcopy(op_hbm.at[:, op_cols(j, cc, t)], op_in.at[t, b * 2 + c],
                               op_s.at[t, kb * 2 + kc], op_r.at[t, kb * 2 + kc], chip_dev(j, cc))
                    cp.start()
                    pend.append(cp)
    for i, (src, dst) in enumerate(((gate_hbm, w4.at[1]), (up_hbm, w4.at[3]), (down_hbm, dn.at[1]))):
        cp = rcopy(src, dst, w_s.at[i], w_r.at[i], sib)
        cp.start()
        pend.append(cp)

    me = z * 2 + yh
    gain_at = (me, pl.ds(ROWS, GROWS), pl.ds(pl.multiple_of(c * FW, FW), FW))
    xg[gain_at] = jnp.broadcast_to(gain_ref[...], (GROWS, FW))
    gain_cp = rcopy(xg.at[gain_at], xg.at[gain_at], g_s, g_r, sib)
    gain_cp.start()
    pend.append(gain_cp)

    ids = idst_ref[...]
    xi = lax.broadcasted_iota(jnp.int32, (16, TOK), 0)
    named = ((ids[0:1] == xi) | (ids[1:2] == xi)).astype(BF16)
    before = (lax.broadcasted_iota(jnp.int32, (TOK, TOK), 0)
              < lax.broadcasted_iota(jnp.int32, (TOK, TOK), 1)).astype(BF16)
    rank = jnp.dot(named, before, preferred_element_type=F32).astype(jnp.int32)
    ci = lax.broadcasted_iota(jnp.int32, (CAP, TOK), 0)
    eye = lax.broadcasted_iota(jnp.int32, (SLOTS, SLOTS), 0) == lax.broadcasted_iota(jnp.int32, (SLOTS, SLOTS), 1)
    table = jnp.sum(jnp.where(eye, table_ref[...], 0.0), axis=1, keepdims=True)
    slot_i = lax.broadcasted_iota(jnp.int32, (SLOTS, TOK), 0)
    raw = [jnp.sum(jnp.where(slots_ref[k:k + 1] == slot_i, table, 0.0), axis=0, keepdims=True) for k in range(2)]
    gates = [raw[k] / (raw[0] + raw[1]) for k in range(2)]
    for x in range(NB):
        hit = rank[x:x + 1] == ci
        first, second = hit & (ids[0:1] == x), hit & (ids[1:2] == x)
        sel[x * CAP:(x + 1) * CAP] = (first | second).astype(BF16)
        gsum[x * CAP:(x + 1) * CAP] = jnp.where(first, gates[0], 0.0) + jnp.where(second, gates[1], 0.0)
    gt = gsum[...].T
    hi = gt.astype(BF16)
    g_hi[...] = hi
    g_lo[...] = (gt - hi.astype(F32)).astype(BF16)
    acc[...] = jnp.zeros_like(acc)
    sq[...] = jnp.zeros_like(sq)

    loads[1].wait()
    for k in range(1, NB):
        src_b = (b + NB - k) % NB
        rcopy(heads_hbm,
              heads_v.at[pl.ds(pl.multiple_of(src_b * TOK, TOK), TOK), pl.ds(pl.multiple_of(c * FW, FW), FW)],
              h_s.at[k - 1], h_r.at[k - 1], sib).wait_recv()
    mine_cols = heads_v.at[:, pl.ds(pl.multiple_of(c * FW, FW), FW)]
    their_cols = heads_v.at[:, pl.ds(pl.multiple_of((1 - c) * FW, FW), FW)]
    cp = rcopy(mine_cols, mine_cols, hf_s, hf_r, sib)
    cp.start()
    pend.append(cp)

    def merge(t):
        loads[2 + t].wait()
        for kb in range(NB):
            for kc in range(2):
                if kb or kc:
                    rcopy(op_hbm.at[:, pl.ds(0, FW)], op_in.at[t, ((b + NB - kb) % NB) * 2 + (c + kc) % 2],
                          op_s.at[t, kb * 2 + kc], op_r.at[t, kb * 2 + kc], sib).wait_recv()
        for cc in range(2):
            total = op_in[t, cc].astype(F32)
            for j in range(1, NB):
                total = total + op_in[t, j * 2 + cc].astype(F32)
            merged[t, cc * FW:(cc + 1) * FW] = (total / NB).astype(BF16)

    def attn_part(zd, t):
        g = (zd + b) % NB
        return jnp.dot(heads_v[pl.ds(pl.multiple_of(g * TOK, TOK), TOK), :], merged[t],
                       preferred_element_type=F32)

    def b_rows(d, u):
        return pl.ds(((d + u) % 2) * 128, 128)

    def b_copy(d, t, s, u):
        rows = b_rows(d, u)
        return rcopy(b_snd.at[d, t, s, rows], b_rcv.at[d, t, s, rows], b_s.at[d, t, s, u], b_r.at[d, t, s, u],
                     dirs[d])

    def start(cp):
        cp.start()
        pend.append(cp)

    def b_first(t):
        p = attn_part((z + 4) % NZ, t)
        for d in range(2):
            b_snd[d, t, 0, b_rows(d, 0)] = p[d * 128:(d + 1) * 128].astype(BF16)
            start(b_copy(d, t, 0, 0))

    def b_step(t, s):
        for d in range(2):
            b_tot[d] = attn_part((z + (4 - s)) % NZ if d == 0 else (z + NZ - (4 - s)) % NZ, t)
        for u in range(2):
            for d in range(2):
                rows = b_rows(d, u)
                if s > 1 or u == 0:
                    b_copy(d, t, s - 1, u).wait_recv()
                    b_snd[d, t, s, rows] = (b_tot[d, rows] + b_rcv[d, t, s - 1, rows].astype(F32)).astype(BF16)
                else:
                    b_snd[d, t, s, rows] = b_tot[d, rows].astype(BF16)
                start(b_copy(d, t, s, u))

    def b_last(t):
        b_tot[0] = attn_part(z, t)
        for u in range(2):
            for d in range(2):
                b_copy(d, t, 3, u).wait_recv()
        return b_tot[0] + b_rcv[0, t, 3].astype(F32) + b_rcv[1, t, 3].astype(F32)

    merge(0)
    rcopy(their_cols, their_cols, hf_s, hf_r, sib).wait_recv()
    b_first(0)
    b_step(0, 1)
    b_step(0, 2)
    merge(1)
    b_first(1)
    b_step(0, 3)
    b_step(1, 1)
    y_snd[...] = b_last(0).astype(BF16)
    y_copy = rcopy(y_snd, y_rcv, yt_s.at[0], yt_r.at[0], ypart)
    start(y_copy)
    b_step(1, 2)
    b_step(1, 3)
    kept = b_last(1)
    y_copy.wait_recv()
    t_snd[...] = (kept + y_rcv[...].astype(F32)).astype(BF16)
    t_copy = rcopy(t_snd, t_rcv, yt_s.at[1], yt_r.at[1], tpart)

    @pl.when(t_self)
    def _():
        t_rcv[...] = t_snd[...]

    @pl.when(jnp.logical_not(t_self))
    def _():
        t_copy.start()
        t_copy.wait_recv()

    loads[0].wait()
    st = res_v[...].astype(F32) + t_rcv[...].astype(F32)
    stream[...] = st
    scaled = (st * gain_ref[...].astype(F32)).astype(BF16)
    dsp[...] = jnp.dot(sel[...], scaled, preferred_element_type=F32).astype(BF16)
    blk_at = (me, pl.ds(pl.multiple_of((b % 4) * CAP, CAP), CAP), pl.ds(pl.multiple_of(c * FW, FW), FW))
    my_src = half == c

    def c_copy(k):
        x = (b + k) % NB
        return rcopy(dsp.at[pl.ds(pl.multiple_of(x * CAP, CAP), CAP)], xg.at[blk_at], c_s.at[k],
                     c_r.at[(b % 4) * 2 + c], chip_dev(x, half))

    own_blk = pltpu.make_async_copy(dsp.at[pl.ds(pl.multiple_of(b * CAP, CAP), CAP)], xg.at[blk_at], loc.at[6])
    for k in range(1, NB):
        c_copy(k).start()
        pend.append(c_copy(k))

    @pl.when(my_src)
    def _():
        own_blk.start()

    @pl.when(jnp.logical_not(my_src))
    def _():
        c_copy(0).start()

    for i in range(8):
        @pl.when(jnp.logical_not(jnp.logical_and(my_src, (b % 4) * 2 + c == i)))
        def _(i=i):
            rcopy(dsp.at[pl.ds(0, CAP)], xg.at[me, pl.ds((i // 2) * CAP, CAP), pl.ds((i % 2) * FW, FW)],
                  c_s.at[0], c_r.at[i], sib).wait_recv()

    @pl.when(my_src)
    def _():
        own_blk.wait()

    sib_gain = xg.at[me, pl.ds(ROWS, GROWS), pl.ds(pl.multiple_of((1 - c) * FW, FW), FW)]
    rcopy(sib_gain, sib_gain, g_s, g_r, sib).wait_recv()

    def ag_copy(d, t, s, slot):
        lo, n = (RD, BLK - RD) if t == 0 else (0, RD)
        if s == 3:
            cut = n // 32 * 16
            lo, n = (lo, cut) if d == 0 else (lo + cut, n - cut)
        ref = xg.at[slot, pl.ds(lo, n)]
        return rcopy(ref, ref, ag_s.at[d, t, s], ag_r.at[d, t, s], dirs[d])

    def agy_copy(i, slot):
        if i == 0:
            lo, n = 0, RD
        elif i < 8:
            lo, n = RD, BLK - RD
        else:
            cut = (BLK - RD) // 32 * 16
            lo, n = (RD, cut) if i == 8 else (RD + cut, BLK - RD - cut)
        ref = xg.at[slot, pl.ds(lo, n)]
        return rcopy(ref, ref, agy_s.at[i], agy_r.at[i], ypart)

    def gate_up(slot):
        blk = xg[slot, 0:ROWS]
        inv = 1.0 / xg[slot, ROWS:BLK][0:1].astype(F32)
        v = blk.astype(F32) * inv
        sq[...] += v * v
        rows = pl.ds(pl.multiple_of(slot * CW, CW), CW)

        def part(i, carry):
            acc[i] += jnp.dot(xg[slot, 0:ROWS], w4[i, rows, :], preferred_element_type=F32)
            return carry
        lax.fori_loop(0, 4, part, 0)

    def slot_of(d, s, t):
        return ((z + NZ - s) % NZ if d == 0 else (z + s) % NZ) * 2 + (yh if t == 0 else 1 - yh)

    other = z * 2 + 1 - yh
    start(agy_copy(0, me))
    for t in range(2):
        for d in range(2):
            start(ag_copy(d, t, 0, me))
        if t == 0:
            start(agy_copy(1, me))
    loads[4].wait()
    loads[5].wait()
    for i in range(2):
        rcopy(gate_hbm, w4.at[1 + 2 * i], w_s.at[i], w_r.at[i], sib).wait_recv()
    gate_up(me)
    agy_copy(0, other).wait_recv()
    for d in range(2):
        start(ag_copy(d, 2, 0, other))
    for s in range(1, 4):
        for t in range(2):
            for d in range(2):
                slot = slot_of(d, s, 0)
                ag_copy(d, t, s - 1, slot).wait_recv()
                start(ag_copy(d, t, s, slot))
                if t == 0:
                    start(agy_copy(2 * s + d, slot))
        gate_up(slot_of(0, s, 0))
        for d in range(2):
            slot = slot_of(d, s, 1)
            ag_copy(d, 2, s - 1, slot).wait_recv()
            start(ag_copy(d, 2, s, slot))
        gate_up(slot_of(1, s, 0))
        if s == 1:
            agy_copy(1, other).wait_recv()
            gate_up(other)
        else:
            for d in range(2):
                slot = slot_of(d, s - 1, 1)
                agy_copy(2 * (s - 1) + d, slot).wait_recv()
                gate_up(slot)
    far = slot_of(0, 4, 0)
    for d in range(2):
        ag_copy(d, 0, 3, far).wait_recv()
        start(agy_copy(8 + d, far))
    for d in range(2):
        ag_copy(d, 1, 3, far).wait_recv()
    gate_up(far)
    for d in range(2):
        slot = slot_of(d, 3, 1)
        agy_copy(6 + d, slot).wait_recv()
        gate_up(slot)
    far = slot_of(0, 4, 1)
    for d in range(2):
        ag_copy(d, 2, 3, far).wait_recv()
        agy_copy(8 + d, far).wait_recv()
    gate_up(far)

    scale = lax.rsqrt(jnp.sum(sq[...], axis=1, keepdims=True) / D + 1e-05)
    for i in range(2):
        g = acc[i] * scale
        hid[i] = (g / (1.0 + jnp.exp(-g)) * (acc[2 + i] * scale)).astype(BF16)
    loads[6].wait()
    rcopy(down_hbm, dn.at[1], w_s.at[2], w_r.at[2], sib).wait_recv()

    def down_part(zd, t):
        yy = 1 - yh if t == 0 else yh
        cols = pl.ds(pl.multiple_of((zd * 2 + yy) * CW, CW), CW)
        return (jnp.dot(hid[0], dn[0, :, cols], preferred_element_type=F32)
                + jnp.dot(hid[1], dn[1, :, cols], preferred_element_type=F32))

    def target(k):
        if k == 0:
            return (z + 4) % NZ
        dist = 4 - (k + 1) // 2
        return (z + dist) % NZ if k % 2 else (z + NZ - dist) % NZ

    def ey_copy(k):
        return rcopy(ey_snd.at[k], ey_rcv.at[k], ey_s.at[k], ey_r.at[k], ypart)

    def e0_copy(d, s):
        rows = pl.ds(d * HALF_1, HALF_1) if s == 0 else pl.ds(0, RE)
        return rcopy(e0_snd.at[d, s, rows], e0_rcv.at[d, s, rows], e_s.at[d, 0, s], e_r.at[d, 0, s], dirs[d])

    def e1_copy(d, t, s):
        lo, n = (0, RE) if t == 1 else (RE, ROWS - RE)
        rows = pl.ds(lo + d * (n // 2), n // 2) if s == 0 else pl.ds(lo, n)
        return rcopy(e1_snd.at[d, s, rows], e1_rcv.at[d, s, rows], e_s.at[d, t, s], e_r.at[d, t, s], dirs[d])

    def other_part(k):
        p = down_part(target(k), 0)
        ey_snd[k] = p[RE:ROWS].astype(BF16)
        start(ey_copy(k))
        e0[k] = p[0:RE]

    other_part(0)
    for d in range(2):
        rows = slice(d * HALF_1, (d + 1) * HALF_1)
        e0_snd[d, 0, rows] = e0[0, rows].astype(BF16)
        start(e0_copy(d, 0))
    e1[0] = down_part(target(0), 1)
    for d in range(2):
        rows = slice(d * HALF_1, (d + 1) * HALF_1)
        e1_snd[d, 0, rows] = e1[0, rows].astype(BF16)
        start(e1_copy(d, 1, 0))
    other_part(1)
    other_part(2)
    ey_copy(0).wait_recv()
    for d in range(2):
        rows = slice(RE + d * HALF_2, RE + (d + 1) * HALF_2)
        e1_snd[d, 0, rows] = (e1[0, rows] + ey_rcv[0, d * HALF_2:(d + 1) * HALF_2].astype(F32)).astype(BF16)
        start(e1_copy(d, 2, 0))
    for s in range(1, 4):
        for d in range(2):
            e1[d] = down_part(target(2 * s - 1 + d), 1)
        for d in range(2):
            k = 2 * s - 1 + d
            e0_copy(d, s - 1).wait_recv()
            if s == 1:
                rows = slice(d * HALF_1, (d + 1) * HALF_1)
                rest = slice((1 - d) * HALF_1, (2 - d) * HALF_1)
                e0_snd[d, s, rows] = (e0[k, rows] + e0_rcv[d, 0, rows].astype(F32)).astype(BF16)
                e0_snd[d, s, rest] = e0[k, rest].astype(BF16)
            else:
                e0_snd[d, s] = (e0[k] + e0_rcv[d, s - 1].astype(F32)).astype(BF16)
            start(e0_copy(d, s))
        for t, lo, n in ((1, 0, RE), (2, RE, ROWS - RE)):
            for d in range(2):
                if t == 2:
                    k = 2 * s - 1 + d
                    ey_copy(k).wait_recv()
                    e1[d, RE:ROWS] += ey_rcv[k].astype(F32)
                e1_copy(d, t, s - 1).wait_recv()
                if s == 1:
                    rows = slice(lo + d * (n // 2), lo + (d + 1) * (n // 2))
                    rest = slice(lo + (1 - d) * (n // 2), lo + (2 - d) * (n // 2))
                    e1_snd[d, s, rows] = (e1[d, rows] + e1_rcv[d, 0, rows].astype(F32)).astype(BF16)
                    e1_snd[d, s, rest] = e1[d, rest].astype(BF16)
                else:
                    rows = slice(lo, lo + n)
                    e1_snd[d, s, rows] = (e1[d, rows] + e1_rcv[d, s - 1, rows].astype(F32)).astype(BF16)
                start(e1_copy(d, t, s))
            if t == 1:
                for d in range(2):
                    if 2 * s + 1 + d < NZ:
                        other_part(2 * s + 1 + d)
    e1[0] = down_part(z, 1)
    for d in range(2):
        e0_copy(d, 3).wait_recv()
    ez_snd[...] = (e0[7] + e0_rcv[0, 3].astype(F32) + e0_rcv[1, 3].astype(F32)).astype(BF16)
    ez = rcopy(ez_snd, ez_rcv, ex_s, ex_r, ypart)
    start(ez)
    ey_copy(7).wait_recv()
    e1[0, RE:ROWS] += ey_rcv[7].astype(F32)
    for t in (1, 2):
        for d in range(2):
            e1_copy(d, t, 3).wait_recv()
    e1[0] = e1[0] + e1_rcv[0, 3].astype(F32) + e1_rcv[1, 3].astype(F32)

    def f_copy(i, cc):
        return rcopy(ret_snd.at[pl.ds(i * CAP, CAP), pl.ds(cc * FW, FW)],
                     ret_v.at[pl.ds(pl.multiple_of(b * CAP, CAP), CAP)],
                     f_s.at[i * 2 + cc], f_r.at[b], chip_dev(4 * c + i, cc))

    for i in (2, 3, 0, 1):
        rows = slice(i * CAP, (i + 1) * CAP)
        if i == 0:
            ez.wait_recv()
            e1[0, 0:RE] += ez_rcv[...].astype(F32)
        ret_snd[rows] = e1[0, rows].astype(BF16)
        for cc in range(2):
            to_self = jnp.logical_and(4 * c + i == b, cc == c)
            mine = pltpu.make_async_copy(ret_snd.at[pl.ds(i * CAP, CAP), pl.ds(cc * FW, FW)],
                                         ret_v.at[pl.ds(pl.multiple_of(b * CAP, CAP), CAP)], loc.at[7])

            @pl.when(to_self)
            def _(mine=mine):
                mine.start()
                mine.wait()

            @pl.when(jnp.logical_not(to_self))
            def _(i=i, cc=cc):
                f_copy(i, cc).start()

    for x in range(NB):
        @pl.when(jnp.logical_not(jnp.logical_and(my_src, b == x)))
        def _(x=x):
            rcopy(ret_snd.at[pl.ds(0, CAP), pl.ds(0, FW)], ret_v.at[pl.ds(x * CAP, CAP)], f_s.at[0], f_r.at[x],
                  sib).wait_recv()
    out_ref[...] = (stream[...] + jnp.dot(g_hi[...], ret_v[...], preferred_element_type=F32)
                    + jnp.dot(g_lo[...], ret_v[...], preferred_element_type=F32)).astype(BF16)

    for cp in pend:
        cp.wait_send()

    @pl.when(jnp.logical_not(t_self))
    def _():
        t_copy.wait_send()

    @pl.when(jnp.logical_not(my_src))
    def _():
        c_copy(0).wait_send()

    for i in range(4):
        for cc in range(2):
            @pl.when(jnp.logical_not(jnp.logical_and(4 * c + i == b, cc == c)))
            def _(i=i, cc=cc):
                f_copy(i, cc).wait_send()


def per_device(residual, heads_out, out_proj, norm_gain, gate_w, up_w, down_w, expert_ids, gate_slots, gate_table):
    any_, vmem = pl.BlockSpec(memory_space=pl.ANY), pl.BlockSpec(memory_space=pltpu.VMEM)
    dma, v = pltpu.SemaphoreType.DMA, pltpu.VMEM
    return pl.pallas_call(
        kernel,
        out_shape=jax.ShapeDtypeStruct((TOK, FW), BF16),
        in_specs=[any_, any_, any_, vmem, any_, any_, any_, vmem, vmem, vmem],
        out_specs=vmem,
        scratch_shapes=[
            v((TOK, FW), BF16), v((NB * TOK, CW), BF16), v((2, 16, FW, FW), BF16), v((2, CW, FW), BF16),
            v((4, D, CW), BF16), v((2, CW, D), BF16), v((NB * CAP, TOK), BF16), v((NB * CAP, TOK), F32),
            v((TOK, NB * CAP), BF16), v((TOK, NB * CAP), BF16),
            v((2, 2, 4, TOK, FW), BF16), v((2, 2, 4, TOK, FW), BF16), v((2, TOK, FW), F32),
            v((TOK, FW), BF16), v((TOK, FW), BF16), v((TOK, FW), BF16), v((TOK, FW), BF16),
            v((TOK, FW), F32), v((NB * CAP, FW), BF16), v((16, BLK, CW), BF16), v((4, ROWS, CW), F32),
            v((ROWS, CW), F32), v((2, ROWS, CW), BF16), v((NZ, RE, CW), F32), v((2, ROWS, CW), F32),
            v((2, 4, RE, CW), BF16), v((2, 4, RE, CW), BF16), v((2, 4, ROWS, CW), BF16), v((2, 4, ROWS, CW), BF16),
            v((NZ, ROWS - RE, CW), BF16), v((NZ, ROWS - RE, CW), BF16), v((RE, CW), BF16), v((RE, CW), BF16),
            v((ROWS, CW), BF16), v((NB * CAP, FW), BF16),
            dma((9,)), dma((3,)), dma((3,)), dma((7,)), dma((7,)), dma, dma, dma((2, 16)), dma((2, 16)),
            dma((2, 2, 4, 2)), dma((2, 2, 4, 2)), dma((2,)), dma((2,)), dma, dma,
            dma((8,)), dma((8,)), dma((2, 3, 4)), dma((2, 3, 4)), dma((10,)), dma((10,)),
            dma((2, 3, 4)), dma((2, 3, 4)), dma, dma, dma((8,)), dma((8,)), dma((8,)), dma((8,)),
        ],
        compiler_params=pltpu.CompilerParams(
            collective_id=0, has_side_effects=True, vmem_limit_bytes=60 * 1024 * 1024),
        name="merge_moe",
    )(residual, heads_out, out_proj[0], norm_gain.reshape(1, FW), gate_w[0], up_w[0], down_w[0],
      expert_ids.T, gate_slots.T, gate_table.reshape(1, SLOTS))


def solution(mesh):
    return jax.shard_map(
        per_device,
        mesh=mesh,
        in_specs=(
            P("branch", "expert"), P("branch", "expert"), P("branch", "expert", None), P("expert"),
            P("branch", None, "expert"), P("branch", None, "expert"), P("branch", "expert", None),
            P("branch", None), P("branch", None), P(),
        ),
        out_specs=P("branch", "expert"),
        check_vma=False,
    )
```

time: 148 us -> 128 us (0.86)
  Pallas kernels: 145 us -> 127 us
    pallas_call x1, Pallas kernels: 145 us -> 127 us  [per_device(): pl.pallas_call(kernel, out_shape=jax.ShapeDtypeStruct((TOK, FW), BF16), i...]
where the time goes in v2:
time: 128 us
  Pallas kernels  127 us (99%)
  local copies, waits for them, and re-layouts  1.47 us (1%)
    pallas_call x1, Pallas kernels, per_device(): pl.pallas_call(kernel, out_shape=jax.ShapeDtypeStruct((TOK, FW), BF16), i...  127 us

profile of v2, /device:TPU:1, one launch (start us, length us, event | category | flops | bytes accessed | tf_op | source)
XLA Modules:
  0.0 128.2 jit_solution(10897596631430723543)
XLA Ops:
  0.0 126.7 %merge_moe.1 = bf16[256,128]{1,0:T(8,128)(2,1)} custom-call(bf16[256,128]{1,0:T(8,128)(2,1)} %res_hbm.1, bf16[256,128]{1,0:T(8,128)(2,1)} %heads_hbm.1, bf16[128,4096]{1,0:T(8,128)(2,1)} %bitcast.11, bf16[1,128]{1,0:T(2,128)(2,1)} %bitcast.14, bf16[4096,256]{1,0:T(8,128)(2,1)} %bitcast.8, bf16[4096,256]{1,0:T(8,128)(2,1)} %bitcast.9, ...), custom_call_target="tpu_custom_call" | custom-call | tf_op jit(solution)/shard_map/merge_moe/pallas_call | solution.py:521
  126.7 1.5 %copy.12 = bf16[256,128]{1,0:T(8,128)(2,1)} copy(bf16[256,128]{1,0:T(8,128)(2,1)} %merge_moe.1) | data formatting | bytes 131072

commit v3 on v2

--- a/solution.py
+++ b/solution.py
@@ -18,6 +18,8 @@
 BLK = ROWS + GROWS
 FW = 128
 CW = 256
+KR = 16
+GROUPS = ((0, 3), (3, 2), (5, 2), (7, 1))
 RD = 176
 RE = 160
 HALF_1, HALF_2 = RE // 2, (ROWS - RE) // 2
@@ -31,10 +33,10 @@
 
 def kernel(res_hbm, heads_hbm, op_hbm, gain_ref, gate_hbm, up_hbm, down_hbm, idst_ref, slots_ref,
            table_ref, out_ref,
-           res_v, heads_v, op_in, merged, w4, dn, sel, gsum, g_hi, g_lo, b_snd, b_rcv, b_tot, y_snd, y_rcv,
-           t_snd, t_rcv, stream, dsp, xg, acc, sq, hid, e0, e1, e0_snd, e0_rcv, e1_snd, e1_rcv, ey_snd, ey_rcv,
+           res_v, heads_v, op_v, op_x, op_in, mg, merged, w4, dn, sel, gsum, g_hi, g_lo, b_snd, b_rcv, b_tot,
+           x_snd, x_rcv, stream, dsp, xg, acc, sq, hid, e0, e1, e0_snd, e0_rcv, e1_snd, e1_rcv, ey_snd, ey_rcv,
            ez_snd, ez_rcv, ret_snd, ret_v,
-           loc, w_s, w_r, h_s, h_r, hf_s, hf_r, op_s, op_r, b_s, b_r, yt_s, yt_r, g_s, g_r,
+           loc, w_s, w_r, h_s, h_r, op_s, op_r, mg_s, mg_r, b_s, b_r, x_s, x_r, g_s, g_r,
            c_s, c_r, ag_s, ag_r, agy_s, agy_r, e_s, e_r, ex_s, ex_r, ey_s, ey_r, f_s, f_r):
     b = lax.axis_index("branch")
     e = lax.axis_index("expert")
@@ -46,27 +48,25 @@
     right = (b, ((z + 1) % NZ) * 4 + yh * 2 + c)
     left = (b, ((z + NZ - 1) % NZ) * 4 + yh * 2 + c)
     ypart = (b, z * 4 + (1 - yh) * 2 + c)
-    grp = (z + b) % NB
-    tpart = (grp, b * 4 + c * 2 + yh)
-    tsrc = (z, ((b + NZ - z) % NZ) * 4 + c * 2 + yh)
-    t_self = (b == 0) & (z == 0) & (yh == c)
+    ydiag = (b, z * 4 + (1 - yh) * 2 + 1 - c)
     dirs = (right, left)
 
     def chip_dev(j, core):
         return (j, z * 4 + yh * 2 + core)
 
-    def op_cols(j, core, t):
-        first = (j * 2 + core) * CW + (1 - yh if t == 0 else yh) * FW
-        return pl.ds(pl.multiple_of(first, FW), FW)
-
+    def target(k):
+        if k == 0:
+            return (z + 4) % NZ
+        if k == NZ - 1:
+            return z
+        dist = 4 - (k + 1) // 2
+        return (z + dist) % NZ if k % 2 else (z + NZ - dist) % NZ
+
+    my_cols = pl.ds(pl.multiple_of(c * FW, FW), FW)
     loads = [
+        pltpu.make_async_copy(op_hbm, op_v, loc.at[2]),
+        pltpu.make_async_copy(heads_hbm, heads_v.at[:, my_cols], loc.at[1]),
         pltpu.make_async_copy(res_hbm, res_v, loc.at[0]),
-        pltpu.make_async_copy(
-            heads_hbm,
-            heads_v.at[pl.ds(pl.multiple_of(b * TOK, TOK), TOK), pl.ds(pl.multiple_of(c * FW, FW), FW)],
-            loc.at[1]),
-        pltpu.make_async_copy(op_hbm.at[:, op_cols(b, c, 0)], op_in.at[0, b * 2 + c], loc.at[2]),
-        pltpu.make_async_copy(op_hbm.at[:, op_cols(b, c, 1)], op_in.at[1, b * 2 + c], loc.at[8]),
         pltpu.make_async_copy(gate_hbm, w4.at[0], loc.at[3]),
         pltpu.make_async_copy(up_hbm, w4.at[2], loc.at[4]),
         pltpu.make_async_copy(down_hbm, dn.at[0], loc.at[5]),
@@ -80,30 +80,63 @@
             if kb or kc:
                 pl.semaphore_signal(barrier, inc=1, device_id=chip_dev((b + kb) % NB, (c + kc) % 2),
                                     device_id_type=MESH)
-    for dev in (right, left, ypart):
+    for dev in (right, left, ypart, ydiag):
         pl.semaphore_signal(barrier, inc=1, device_id=dev, device_id_type=MESH)
 
-    @pl.when(jnp.logical_not(t_self))
-    def _():
-        pl.semaphore_signal(barrier, inc=1, device_id=tsrc, device_id_type=MESH)
-
-    pl.semaphore_wait(barrier, jnp.where(t_self, 18, 19))
+    loads[0].wait()
+    for k in range(NZ):
+        for cc in range(2):
+            cols = pl.ds(pl.multiple_of(target(k) * 2 * CW + cc * CW, CW), CW)
+            op_x[:, cc, k] = op_v[:, cols].reshape(NB, KR, CW)
+    op_in[b * 2 + c] = op_x[b, c]
+    pl.semaphore_wait(barrier, 19)
 
     pend = []
-    my_heads = heads_v.at[pl.ds(pl.multiple_of(b * TOK, TOK), TOK), pl.ds(pl.multiple_of(c * FW, FW), FW)]
-    for k in range(1, NB):
-        cp = rcopy(heads_hbm, my_heads, h_s.at[k - 1], h_r.at[k - 1], chip_dev((b + k) % NB, c))
+
+    def start(cp):
         cp.start()
         pend.append(cp)
-    for t in range(2):
+
+    def op_send(i):
+        q, n = GROUPS[i]
         for kb in range(NB):
             for kc in range(2):
                 if kb or kc:
                     j, cc = (b + kb) % NB, (c + kc) % 2
-                    cp = rcopy(op_hbm.at[:, op_cols(j, cc, t)], op_in.at[t, b * 2 + c],
-                               op_s.at[t, kb * 2 + kc], op_r.at[t, kb * 2 + kc], chip_dev(j, cc))
-                    cp.start()
-                    pend.append(cp)
+                    start(rcopy(op_x.at[j, cc, pl.ds(q, n)], op_in.at[b * 2 + c, pl.ds(q, n)],
+                                op_s.at[i, kb * 2 + kc], op_r.at[i, kb * 2 + kc], chip_dev(j, cc)))
+
+    def mg_copy(i, k, j):
+        q, n = GROUPS[i]
+        return rcopy(mg.at[pl.ds(q, n)], merged.at[pl.ds(q, n), :, pl.ds(pl.multiple_of(j * KR, KR), KR)],
+                     mg_s.at[i, k - 1], mg_r.at[i, k - 1], chip_dev((b + k) % NB, c))
+
+    def merge(i):
+        q, n = GROUPS[i]
+        for kb in range(NB):
+            for kc in range(2):
+                if kb or kc:
+                    rcopy(op_x.at[0, 0, pl.ds(q, n)],
+                          op_in.at[((b + NB - kb) % NB) * 2 + (c + kc) % 2, pl.ds(q, n)],
+                          op_s.at[i, kb * 2 + kc], op_r.at[i, kb * 2 + kc], sib).wait_recv()
+        for k in range(q, q + n):
+            for cc in range(2):
+                total = op_in[cc, k].astype(F32)
+                for j in range(1, NB):
+                    total = total + op_in[j * 2 + cc, k].astype(F32)
+                total = (total / NB).astype(BF16)
+                mg[k, cc] = total
+                merged[k, cc, pl.ds(pl.multiple_of(b * KR, KR), KR)] = total
+        for k in range(1, NB):
+            start(mg_copy(i, k, b))
+
+    def merged_wait(i):
+        for k in range(1, NB):
+            mg_copy(i, k, (b + NB - k) % NB).wait_recv()
+
+    op_send(0)
+    start(rcopy(heads_hbm, heads_v.at[:, my_cols], h_s, h_r, sib))
+    op_send(1)
     for i, (src, dst) in enumerate(((gate_hbm, w4.at[1]), (up_hbm, w4.at[3]), (down_hbm, dn.at[1]))):
         cp = rcopy(src, dst, w_s.at[i], w_r.at[i], sib)
         cp.start()
@@ -140,104 +173,78 @@
     acc[...] = jnp.zeros_like(acc)
     sq[...] = jnp.zeros_like(sq)
 
-    loads[1].wait()
-    for k in range(1, NB):
-        src_b = (b + NB - k) % NB
-        rcopy(heads_hbm,
-              heads_v.at[pl.ds(pl.multiple_of(src_b * TOK, TOK), TOK), pl.ds(pl.multiple_of(c * FW, FW), FW)],
-              h_s.at[k - 1], h_r.at[k - 1], sib).wait_recv()
-    mine_cols = heads_v.at[:, pl.ds(pl.multiple_of(c * FW, FW), FW)]
-    their_cols = heads_v.at[:, pl.ds(pl.multiple_of((1 - c) * FW, FW), FW)]
-    cp = rcopy(mine_cols, mine_cols, hf_s, hf_r, sib)
-    cp.start()
-    pend.append(cp)
-
-    def merge(t):
-        loads[2 + t].wait()
-        for kb in range(NB):
-            for kc in range(2):
-                if kb or kc:
-                    rcopy(op_hbm.at[:, pl.ds(0, FW)], op_in.at[t, ((b + NB - kb) % NB) * 2 + (c + kc) % 2],
-                          op_s.at[t, kb * 2 + kc], op_r.at[t, kb * 2 + kc], sib).wait_recv()
-        for cc in range(2):
-            total = op_in[t, cc].astype(F32)
-            for j in range(1, NB):
-                total = total + op_in[t, j * 2 + cc].astype(F32)
-            merged[t, cc * FW:(cc + 1) * FW] = (total / NB).astype(BF16)
-
-    def attn_part(zd, t):
-        g = (zd + b) % NB
-        return jnp.dot(heads_v[pl.ds(pl.multiple_of(g * TOK, TOK), TOK), :], merged[t],
-                       preferred_element_type=F32)
+    def attn_part(k):
+        return jnp.dot(heads_v[...], merged[k].reshape(CW, CW), preferred_element_type=F32)
 
     def b_rows(d, u):
         return pl.ds(((d + u) % 2) * 128, 128)
 
-    def b_copy(d, t, s, u):
+    def b_copy(d, s, u):
         rows = b_rows(d, u)
-        return rcopy(b_snd.at[d, t, s, rows], b_rcv.at[d, t, s, rows], b_s.at[d, t, s, u], b_r.at[d, t, s, u],
-                     dirs[d])
-
-    def start(cp):
-        cp.start()
-        pend.append(cp)
-
-    def b_first(t):
-        p = attn_part((z + 4) % NZ, t)
-        for d in range(2):
-            b_snd[d, t, 0, b_rows(d, 0)] = p[d * 128:(d + 1) * 128].astype(BF16)
-            start(b_copy(d, t, 0, 0))
-
-    def b_step(t, s):
-        for d in range(2):
-            b_tot[d] = attn_part((z + (4 - s)) % NZ if d == 0 else (z + NZ - (4 - s)) % NZ, t)
+        return rcopy(b_snd.at[d, s, rows], b_rcv.at[d, s, rows], b_s.at[d, s, u], b_r.at[d, s, u], dirs[d])
+
+    def b_step(s):
+        for d in range(2):
+            b_tot[d] = attn_part(2 * s - 1 + d)
         for u in range(2):
             for d in range(2):
                 rows = b_rows(d, u)
                 if s > 1 or u == 0:
-                    b_copy(d, t, s - 1, u).wait_recv()
-                    b_snd[d, t, s, rows] = (b_tot[d, rows] + b_rcv[d, t, s - 1, rows].astype(F32)).astype(BF16)
+                    b_copy(d, s - 1, u).wait_recv()
+                    b_snd[d, s, rows] = (b_tot[d, rows] + b_rcv[d, s - 1, rows].astype(F32)).astype(BF16)
                 else:
-                    b_snd[d, t, s, rows] = b_tot[d, rows].astype(BF16)
-                start(b_copy(d, t, s, u))
-
-    def b_last(t):
-        b_tot[0] = attn_part(z, t)
-        for u in range(2):
-            for d in range(2):
-                b_copy(d, t, 3, u).wait_recv()
-        return b_tot[0] + b_rcv[0, t, 3].astype(F32) + b_rcv[1, t, 3].astype(F32)
+                    b_snd[d, s, rows] = b_tot[d, rows].astype(BF16)
+                start(b_copy(d, s, u))
 
     merge(0)
-    rcopy(their_cols, their_cols, hf_s, hf_r, sib).wait_recv()
-    b_first(0)
-    b_step(0, 1)
-    b_step(0, 2)
+    op_send(2)
     merge(1)
-    b_first(1)
-    b_step(0, 3)
-    b_step(1, 1)
-    y_snd[...] = b_last(0).astype(BF16)
-    y_copy = rcopy(y_snd, y_rcv, yt_s.at[0], yt_r.at[0], ypart)
-    start(y_copy)
-    b_step(1, 2)
-    b_step(1, 3)
-    kept = b_last(1)
-    y_copy.wait_recv()
-    t_snd[...] = (kept + y_rcv[...].astype(F32)).astype(BF16)
-    t_copy = rcopy(t_snd, t_rcv, yt_s.at[1], yt_r.at[1], tpart)
-
-    @pl.when(t_self)
+    op_send(3)
+    loads[1].wait()
+    their_cols = heads_v.at[:, pl.ds(pl.multiple_of((1 - c) * FW, FW), FW)]
+    rcopy(their_cols, their_cols, h_s, h_r, sib).wait_recv()
+    merged_wait(0)
+    p = attn_part(0)
+    for d in range(2):
+        b_snd[d, 0, b_rows(d, 0)] = p[d * 128:(d + 1) * 128].astype(BF16)
+        start(b_copy(d, 0, 0))
+    merge(2)
+    b_step(1)
+    merge(3)
+    merged_wait(1)
+    b_step(2)
+    merged_wait(2)
+    b_step(3)
+    merged_wait(3)
+    b_tot[0] = attn_part(NZ - 1)
+    for u in range(2):
+        for d in range(2):
+            b_copy(d, 3, u).wait_recv()
+    x_snd[...] = (b_tot[0] + b_rcv[0, 3].astype(F32) + b_rcv[1, 3].astype(F32)).astype(BF16)
+
+    def x_copy(w):
+        return rcopy(x_snd.at[:, pl.ds(w * FW, FW)], x_rcv.at[jnp.where(yh == c, 0, 1)], x_s.at[w],
+                     x_r.at[jnp.where(yh == c, 0, 1)], (b, z * 4 + c * 2 + w))
+
+    for w in range(2):
+        keep = (yh == c) & (c == w)
+
+        @pl.when(keep)
+        def _(w=w):
+            x_rcv[0] = x_snd[:, w * FW:(w + 1) * FW]
+
+        @pl.when(jnp.logical_not(keep))
+        def _(w=w):
+            x_copy(w).start()
+
+    @pl.when(yh != c)
     def _():
-        t_rcv[...] = t_snd[...]
-
-    @pl.when(jnp.logical_not(t_self))
-    def _():
-        t_copy.start()
-        t_copy.wait_recv()
-
-    loads[0].wait()
-    st = res_v[...].astype(F32) + t_rcv[...].astype(F32)
+        rcopy(x_rcv.at[0], x_rcv.at[0], x_s.at[0], x_r.at[0], sib).wait_recv()
+
+    rcopy(x_rcv.at[1], x_rcv.at[1], x_s.at[0], x_r.at[1], sib).wait_recv()
+
+    loads[2].wait()
+    st = res_v[...].astype(F32) + (x_rcv[0].astype(F32) + x_rcv[1].astype(F32))
     stream[...] = st
     scaled = (st * gain_ref[...].astype(F32)).astype(BF16)
     dsp[...] = jnp.dot(sel[...], scaled, preferred_element_type=F32).astype(BF16)
@@ -316,8 +323,8 @@
             start(ag_copy(d, t, 0, me))
         if t == 0:
             start(agy_copy(1, me))
+    loads[3].wait()
     loads[4].wait()
-    loads[5].wait()
     for i in range(2):
         rcopy(gate_hbm, w4.at[1 + 2 * i], w_s.at[i], w_r.at[i], sib).wait_recv()
     gate_up(me)
@@ -367,7 +374,7 @@
     for i in range(2):
         g = acc[i] * scale
         hid[i] = (g / (1.0 + jnp.exp(-g)) * (acc[2 + i] * scale)).astype(BF16)
-    loads[6].wait()
+    loads[5].wait()
     rcopy(down_hbm, dn.at[1], w_s.at[2], w_r.at[2], sib).wait_recv()
 
     def down_part(zd, t):
@@ -375,12 +382,6 @@
         cols = pl.ds(pl.multiple_of((zd * 2 + yy) * CW, CW), CW)
         return (jnp.dot(hid[0], dn[0, :, cols], preferred_element_type=F32)
                 + jnp.dot(hid[1], dn[1, :, cols], preferred_element_type=F32))
-
-    def target(k):
-        if k == 0:
-            return (z + 4) % NZ
-        dist = 4 - (k + 1) // 2
-        return (z + dist) % NZ if k % 2 else (z + NZ - dist) % NZ
 
     def ey_copy(k):
         return rcopy(ey_snd.at[k], ey_rcv.at[k], ey_s.at[k], ey_r.at[k], ypart)
@@ -500,9 +501,10 @@
     for cp in pend:
         cp.wait_send()
 
-    @pl.when(jnp.logical_not(t_self))
-    def _():
-        t_copy.wait_send()
+    for w in range(2):
+        @pl.when(jnp.logical_not((yh == c) & (c == w)))
+        def _(w=w):
+            x_copy(w).wait_send()
 
     @pl.when(jnp.logical_not(my_src))
     def _():
@@ -524,18 +526,19 @@
         in_specs=[any_, any_, any_, vmem, any_, any_, any_, vmem, vmem, vmem],
         out_specs=vmem,
         scratch_shapes=[
-            v((TOK, FW), BF16), v((NB * TOK, CW), BF16), v((2, 16, FW, FW), BF16), v((2, CW, FW), BF16),
+            v((TOK, FW), BF16), v((TOK, CW), BF16), v((FW, D), BF16), v((NB, 2, NZ, KR, CW), BF16),
+            v((16, NZ, KR, CW), BF16), v((NZ, 2, KR, CW), BF16), v((NZ, 2, FW, CW), BF16),
             v((4, D, CW), BF16), v((2, CW, D), BF16), v((NB * CAP, TOK), BF16), v((NB * CAP, TOK), F32),
             v((TOK, NB * CAP), BF16), v((TOK, NB * CAP), BF16),
-            v((2, 2, 4, TOK, FW), BF16), v((2, 2, 4, TOK, FW), BF16), v((2, TOK, FW), F32),
-            v((TOK, FW), BF16), v((TOK, FW), BF16), v((TOK, FW), BF16), v((TOK, FW), BF16),
+            v((2, 4, TOK, CW), BF16), v((2, 4, TOK, CW), BF16), v((2, TOK, CW), F32),
+            v((TOK, CW), BF16), v((2, TOK, FW), BF16),
             v((TOK, FW), F32), v((NB * CAP, FW), BF16), v((16, BLK, CW), BF16), v((4, ROWS, CW), F32),
             v((ROWS, CW), F32), v((2, ROWS, CW), BF16), v((NZ, RE, CW), F32), v((2, ROWS, CW), F32),
             v((2, 4, RE, CW), BF16), v((2, 4, RE, CW), BF16), v((2, 4, ROWS, CW), BF16), v((2, 4, ROWS, CW), BF16),
             v((NZ, ROWS - RE, CW), BF16), v((NZ, ROWS - RE, CW), BF16), v((RE, CW), BF16), v((RE, CW), BF16),
             v((ROWS, CW), BF16), v((NB * CAP, FW), BF16),
-            dma((9,)), dma((3,)), dma((3,)), dma((7,)), dma((7,)), dma, dma, dma((2, 16)), dma((2, 16)),
-            dma((2, 2, 4, 2)), dma((2, 2, 4, 2)), dma((2,)), dma((2,)), dma, dma,
+            dma((9,)), dma((3,)), dma((3,)), dma, dma, dma((4, 16)), dma((4, 16)), dma((4, 7)), dma((4, 7)),
+            dma((2, 4, 2)), dma((2, 4, 2)), dma((2,)), dma((2,)), dma, dma,
             dma((8,)), dma((8,)), dma((2, 3, 4)), dma((2, 3, 4)), dma((10,)), dma((10,)),
             dma((2, 3, 4)), dma((2, 3, 4)), dma, dma, dma((8,)), dma((8,)), dma((8,)), dma((8,)),
         ],

time: 128 us -> 121 us (0.945)
  Pallas kernels: 127 us -> 120 us
    pallas_call x1, Pallas kernels: 127 us -> 120 us  [per_device(): pl.pallas_call(kernel, out_shape=jax.ShapeDtypeStruct((TOK, FW), BF16), i...]
where the time goes in v3:
time: 121 us
  Pallas kernels  120 us (99%)
  local copies, waits for them, and re-layouts  1.47 us (1%)
    pallas_call x1, Pallas kernels, per_device(): pl.pallas_call(kernel, out_shape=jax.ShapeDtypeStruct((TOK, FW), BF16), i...  120 us

profile of v3, /device:TPU:1, one launch (start us, length us, event | category | flops | bytes accessed | tf_op | source)
XLA Modules:
  0.0 121.1 jit_solution(6997974209557445029)
XLA Ops:
  0.0 119.6 %merge_moe.1 = bf16[256,128]{1,0:T(8,128)(2,1)} custom-call(bf16[256,128]{1,0:T(8,128)(2,1)} %res_hbm.1, bf16[256,128]{1,0:T(8,128)(2,1)} %heads_hbm.1, bf16[128,4096]{1,0:T(8,128)(2,1)} %bitcast.11, bf16[1,128]{1,0:T(2,128)(2,1)} %bitcast.14, bf16[4096,256]{1,0:T(8,128)(2,1)} %bitcast.8, bf16[4096,256]{1,0:T(8,128)(2,1)} %bitcast.9, ...), custom_call_target="tpu_custom_call" | custom-call | tf_op jit(solution)/shard_map/merge_moe/pallas_call | solution.py:523
  119.6 1.5 %copy.12 = bf16[256,128]{1,0:T(8,128)(2,1)} copy(bf16[256,128]{1,0:T(8,128)(2,1)} %merge_moe.1) | data formatting | bytes 131072

commit v4 on v3

--- a/solution.py
+++ b/solution.py
@@ -20,7 +20,7 @@
 CW = 256
 KR = 16
 GROUPS = ((0, 3), (3, 2), (5, 2), (7, 1))
-RD = 176
+RD = 144
 RE = 160
 HALF_1, HALF_2 = RE // 2, (ROWS - RE) // 2
 
@@ -80,7 +80,8 @@
             if kb or kc:
                 pl.semaphore_signal(barrier, inc=1, device_id=chip_dev((b + kb) % NB, (c + kc) % 2),
                                     device_id_type=MESH)
-    for dev in (right, left, ypart, ydiag):
+    ring_devs = [(b, ((z + dz) % NZ) * 4 + i) for dz in (1, NZ - 1) for i in range(4)]
+    for dev in ring_devs + [ypart, ydiag]:
         pl.semaphore_signal(barrier, inc=1, device_id=dev, device_id_type=MESH)
 
     loads[0].wait()
@@ -89,7 +90,7 @@
             cols = pl.ds(pl.multiple_of(target(k) * 2 * CW + cc * CW, CW), CW)
             op_x[:, cc, k] = op_v[:, cols].reshape(NB, KR, CW)
     op_in[b * 2 + c] = op_x[b, c]
-    pl.semaphore_wait(barrier, 19)
+    pl.semaphore_wait(barrier, 25)
 
     pend = []
 
@@ -183,6 +184,18 @@
         rows = b_rows(d, u)
         return rcopy(b_snd.at[d, s, rows], b_rcv.at[d, s, rows], b_s.at[d, s, u], b_r.at[d, s, u], dirs[d])
 
+    def x_copy(kind, w, u):
+        rows = pl.ds(u * 128, 128) if kind == 2 else b_rows(kind, u)
+        src = x_snd.at[rows, pl.ds(w * FW, FW)] if kind == 2 else b_snd.at[kind, 3, rows, pl.ds(w * FW, FW)]
+        zt = ((z + 1) % NZ, (z + NZ - 1) % NZ, z)[kind]
+        return rcopy(src, x_rcv.at[kind, yh, rows], x_s.at[kind, w, u], x_r.at[kind, yh, u],
+                     (b, zt * 4 + c * 2 + w))
+
+    def x_wait(kind, ys, u):
+        rows = pl.ds(u * 128, 128) if kind == 2 else b_rows(kind, u)
+        ref = x_rcv.at[kind, ys, rows]
+        rcopy(ref, ref, x_s.at[0, 0, 0], x_r.at[kind, ys, u], sib).wait_recv()
+
     def b_step(s):
         for d in range(2):
             b_tot[d] = attn_part(2 * s - 1 + d)
@@ -194,7 +207,11 @@
                     b_snd[d, s, rows] = (b_tot[d, rows] + b_rcv[d, s - 1, rows].astype(F32)).astype(BF16)
                 else:
                     b_snd[d, s, rows] = b_tot[d, rows].astype(BF16)
-                start(b_copy(d, s, u))
+                if s < 3:
+                    start(b_copy(d, s, u))
+                else:
+                    for w in range(2):
+                        start(x_copy(d, w, u))
 
     merge(0)
     op_send(2)
@@ -216,35 +233,34 @@
     merged_wait(2)
     b_step(3)
     merged_wait(3)
-    b_tot[0] = attn_part(NZ - 1)
+    x_snd[...] = attn_part(NZ - 1).astype(BF16)
     for u in range(2):
-        for d in range(2):
-            b_copy(d, 3, u).wait_recv()
-    x_snd[...] = (b_tot[0] + b_rcv[0, 3].astype(F32) + b_rcv[1, 3].astype(F32)).astype(BF16)
-
-    def x_copy(w):
-        return rcopy(x_snd.at[:, pl.ds(w * FW, FW)], x_rcv.at[jnp.where(yh == c, 0, 1)], x_s.at[w],
-                     x_r.at[jnp.where(yh == c, 0, 1)], (b, z * 4 + c * 2 + w))
-
-    for w in range(2):
-        keep = (yh == c) & (c == w)
-
-        @pl.when(keep)
-        def _(w=w):
-            x_rcv[0] = x_snd[:, w * FW:(w + 1) * FW]
-
-        @pl.when(jnp.logical_not(keep))
-        def _(w=w):
-            x_copy(w).start()
-
-    @pl.when(yh != c)
-    def _():
-        rcopy(x_rcv.at[0], x_rcv.at[0], x_s.at[0], x_r.at[0], sib).wait_recv()
-
-    rcopy(x_rcv.at[1], x_rcv.at[1], x_s.at[0], x_r.at[1], sib).wait_recv()
+        for w in range(2):
+            keep = (yh == c) & (c == w)
+
+            @pl.when(keep)
+            def _(u=u, w=w):
+                x_rcv[2, yh, u * 128:(u + 1) * 128] = x_snd[u * 128:(u + 1) * 128, w * FW:(w + 1) * FW]
+
+            @pl.when(jnp.logical_not(keep))
+            def _(u=u, w=w):
+                x_copy(2, w, u).start()
+
+    for u in range(2):
+        for kind in range(2):
+            for ys in range(2):
+                x_wait(kind, ys, u)
+    for ys in range(2):
+        @pl.when(jnp.logical_not((yh == c) & (yh == ys)))
+        def _(ys=ys):
+            for u in range(2):
+                x_wait(2, ys, u)
 
     loads[2].wait()
-    st = res_v[...].astype(F32) + (x_rcv[0].astype(F32) + x_rcv[1].astype(F32))
+    attn = x_rcv[0, 0].astype(F32)
+    for i in range(1, 6):
+        attn = attn + x_rcv[i // 2, i % 2].astype(F32)
+    st = res_v[...].astype(F32) + attn
     stream[...] = st
     scaled = (st * gain_ref[...].astype(F32)).astype(BF16)
     dsp[...] = jnp.dot(sel[...], scaled, preferred_element_type=F32).astype(BF16)
@@ -504,7 +520,8 @@
     for w in range(2):
         @pl.when(jnp.logical_not((yh == c) & (c == w)))
         def _(w=w):
-            x_copy(w).wait_send()
+            for u in range(2):
+                x_copy(2, w, u).wait_send()
 
     @pl.when(jnp.logical_not(my_src))
     def _():
@@ -531,14 +548,14 @@
             v((4, D, CW), BF16), v((2, CW, D), BF16), v((NB * CAP, TOK), BF16), v((NB * CAP, TOK), F32),
             v((TOK, NB * CAP), BF16), v((TOK, NB * CAP), BF16),
             v((2, 4, TOK, CW), BF16), v((2, 4, TOK, CW), BF16), v((2, TOK, CW), F32),
-            v((TOK, CW), BF16), v((2, TOK, FW), BF16),
+            v((TOK, CW), BF16), v((3, 2, TOK, FW), BF16),
             v((TOK, FW), F32), v((NB * CAP, FW), BF16), v((16, BLK, CW), BF16), v((4, ROWS, CW), F32),
             v((ROWS, CW), F32), v((2, ROWS, CW), BF16), v((NZ, RE, CW), F32), v((2, ROWS, CW), F32),
             v((2, 4, RE, CW), BF16), v((2, 4, RE, CW), BF16), v((2, 4, ROWS, CW), BF16), v((2, 4, ROWS, CW), BF16),
             v((NZ, ROWS - RE, CW), BF16), v((NZ, ROWS - RE, CW), BF16), v((RE, CW), BF16), v((RE, CW), BF16),
             v((ROWS, CW), BF16), v((NB * CAP, FW), BF16),
             dma((9,)), dma((3,)), dma((3,)), dma, dma, dma((4, 16)), dma((4, 16)), dma((4, 7)), dma((4, 7)),
-            dma((2, 4, 2)), dma((2, 4, 2)), dma((2,)), dma((2,)), dma, dma,
+            dma((2, 3, 2)), dma((2, 3, 2)), dma((3, 2, 2)), dma((3, 2, 2)), dma, dma,
             dma((8,)), dma((8,)), dma((2, 3, 4)), dma((2, 3, 4)), dma((10,)), dma((10,)),
             dma((2, 3, 4)), dma((2, 3, 4)), dma, dma, dma((8,)), dma((8,)), dma((8,)), dma((8,)),
         ],

time: 121 us -> 118 us (0.975)
  Pallas kernels: 120 us -> 116 us
    pallas_call x1, Pallas kernels: 120 us -> 116 us  [per_device(): pl.pallas_call(kernel, out_shape=jax.ShapeDtypeStruct((TOK, FW), BF16), i...]
where the time goes in v4:
time: 118 us
  Pallas kernels  116 us (98%)
  local copies, waits for them, and re-layouts  1.47 us (1%)
    pallas_call x1, Pallas kernels, per_device(): pl.pallas_call(kernel, out_shape=jax.ShapeDtypeStruct((TOK, FW), BF16), i...  116 us

profile of v4, /device:TPU:1, one launch (start us, length us, event | category | flops | bytes accessed | tf_op | source)
XLA Modules:
  0.0 117.7 jit_solution(6447154500970702413)
XLA Ops:
  0.0 116.2 %merge_moe.1 = bf16[256,128]{1,0:T(8,128)(2,1)} custom-call(bf16[256,128]{1,0:T(8,128)(2,1)} %res_hbm.1, bf16[256,128]{1,0:T(8,128)(2,1)} %heads_hbm.1, bf16[128,4096]{1,0:T(8,128)(2,1)} %bitcast.11, bf16[1,128]{1,0:T(2,128)(2,1)} %bitcast.14, bf16[4096,256]{1,0:T(8,128)(2,1)} %bitcast.8, bf16[4096,256]{1,0:T(8,128)(2,1)} %bitcast.9, ...), custom_call_target="tpu_custom_call" | custom-call | tf_op jit(solution)/shard_map/merge_moe/pallas_call | solution.py:540
  116.2 1.5 %copy.12 = bf16[256,128]{1,0:T(8,128)(2,1)} copy(bf16[256,128]{1,0:T(8,128)(2,1)} %merge_moe.1) | data formatting | bytes 131072

commit v5 on v4

--- a/solution.py
+++ b/solution.py
@@ -19,7 +19,7 @@
 FW = 128
 CW = 256
 KR = 16
-GROUPS = ((0, 3), (3, 2), (5, 2), (7, 1))
+GROUPS = ((0, 1), (1, 2), (3, 2), (5, 2), (7, 1))
 RD = 144
 RE = 160
 HALF_1, HALF_2 = RE // 2, (ROWS - RE) // 2
@@ -226,13 +226,16 @@
         b_snd[d, 0, b_rows(d, 0)] = p[d * 128:(d + 1) * 128].astype(BF16)
         start(b_copy(d, 0, 0))
     merge(2)
+    op_send(4)
+    merged_wait(1)
     b_step(1)
     merge(3)
-    merged_wait(1)
+    merged_wait(2)
     b_step(2)
-    merged_wait(2)
+    merge(4)
+    merged_wait(3)
     b_step(3)
-    merged_wait(3)
+    merged_wait(4)
     x_snd[...] = attn_part(NZ - 1).astype(BF16)
     for u in range(2):
         for w in range(2):
@@ -554,7 +557,7 @@
             v((2, 4, RE, CW), BF16), v((2, 4, RE, CW), BF16), v((2, 4, ROWS, CW), BF16), v((2, 4, ROWS, CW), BF16),
             v((NZ, ROWS - RE, CW), BF16), v((NZ, ROWS - RE, CW), BF16), v((RE, CW), BF16), v((RE, CW), BF16),
             v((ROWS, CW), BF16), v((NB * CAP, FW), BF16),
-            dma((9,)), dma((3,)), dma((3,)), dma, dma, dma((4, 16)), dma((4, 16)), dma((4, 7)), dma((4, 7)),
+            dma((9,)), dma((3,)), dma((3,)), dma, dma, dma((5, 16)), dma((5, 16)), dma((5, 7)), dma((5, 7)),
             dma((2, 3, 2)), dma((2, 3, 2)), dma((3, 2, 2)), dma((3, 2, 2)), dma, dma,
             dma((8,)), dma((8,)), dma((2, 3, 4)), dma((2, 3, 4)), dma((10,)), dma((10,)),
             dma((2, 3, 4)), dma((2, 3, 4)), dma, dma, dma((8,)), dma((8,)), dma((8,)), dma((8,)),

time: 118 us -> 116 us (0.983)
    pallas_call x1, Pallas kernels: 116 us -> 115 us  [per_device(): pl.pallas_call(kernel, out_shape=jax.ShapeDtypeStruct((TOK, FW), BF16), i...]
where the time goes in v5:
time: 116 us
  Pallas kernels  115 us (99%)
  local copies, waits for them, and re-layouts  1.47 us (1%)
    pallas_call x1, Pallas kernels, per_device(): pl.pallas_call(kernel, out_shape=jax.ShapeDtypeStruct((TOK, FW), BF16), i...  115 us

profile of v5, /device:TPU:1, one launch (start us, length us, event | category | flops | bytes accessed | tf_op | source)
XLA Modules:
  0.0 116.1 jit_solution(4000762184487481050)
XLA Ops:
  0.0 114.6 %merge_moe.1 = bf16[256,128]{1,0:T(8,128)(2,1)} custom-call(bf16[256,128]{1,0:T(8,128)(2,1)} %res_hbm.1, bf16[256,128]{1,0:T(8,128)(2,1)} %heads_hbm.1, bf16[128,4096]{1,0:T(8,128)(2,1)} %bitcast.11, bf16[1,128]{1,0:T(2,128)(2,1)} %bitcast.14, bf16[4096,256]{1,0:T(8,128)(2,1)} %bitcast.8, bf16[4096,256]{1,0:T(8,128)(2,1)} %bitcast.9, ...), custom_call_target="tpu_custom_call" | custom-call | tf_op jit(solution)/shard_map/merge_moe/pallas_call | solution.py:543
  114.6 1.5 %copy.12 = bf16[256,128]{1,0:T(8,128)(2,1)} copy(bf16[256,128]{1,0:T(8,128)(2,1)} %merge_moe.1) | data formatting | bytes 131072

commit v6 on v5

--- a/solution.py
+++ b/solution.py
@@ -97,6 +97,11 @@
     def start(cp):
         cp.start()
         pend.append(cp)
+
+    def drain():
+        for cp in pend:
+            cp.wait_send()
+        pend.clear()
 
     def op_send(i):
         q, n = GROUPS[i]
@@ -346,6 +351,9 @@
     loads[4].wait()
     for i in range(2):
         rcopy(gate_hbm, w4.at[1 + 2 * i], w_s.at[i], w_r.at[i], sib).wait_recv()
+    drain_a, pend[:] = pend[:-9], pend[-9:]
+    for cp in drain_a:
+        cp.wait_send()
     gate_up(me)
     agy_copy(0, other).wait_recv()
     for d in range(2):
@@ -471,6 +479,9 @@
                 for d in range(2):
                     if 2 * s + 1 + d < NZ:
                         other_part(2 * s + 1 + d)
+    drain_e, pend[:] = pend[:-6], pend[-6:]
+    for cp in drain_e:
+        cp.wait_send()
     e1[0] = down_part(z, 1)
     for d in range(2):
         e0_copy(d, 3).wait_recv()
@@ -509,6 +520,7 @@
             def _(i=i, cc=cc):
                 f_copy(i, cc).start()
 
+    drain()
     for x in range(NB):
         @pl.when(jnp.logical_not(jnp.logical_and(my_src, b == x)))
         def _(x=x):
@@ -516,9 +528,6 @@
                   sib).wait_recv()
     out_ref[...] = (stream[...] + jnp.dot(g_hi[...], ret_v[...], preferred_element_type=F32)
                     + jnp.dot(g_lo[...], ret_v[...], preferred_element_type=F32)).astype(BF16)
-
-    for cp in pend:
-        cp.wait_send()
 
     for w in range(2):
         @pl.when(jnp.logical_not((yh == c) & (c == w)))

time: 116 us -> 116 us (level)
  no operation moved by 1% of the time
where the time goes in v6:
time: 116 us
  Pallas kernels  114 us (98%)
  local copies, waits for them, and re-layouts  1.47 us (1%)
    pallas_call x1, Pallas kernels, per_device(): pl.pallas_call(kernel, out_shape=jax.ShapeDtypeStruct((TOK, FW), BF16), i...  114 us

profile of v6, /device:TPU:1, one launch (start us, length us, event | category | flops | bytes accessed | tf_op | source)
XLA Modules:
  0.0 115.6 jit_solution(6380875484109149569)
XLA Ops:
  0.0 114.1 %merge_moe.1 = bf16[256,128]{1,0:T(8,128)(2,1)} custom-call(bf16[256,128]{1,0:T(8,128)(2,1)} %res_hbm.1, bf16[256,128]{1,0:T(8,128)(2,1)} %heads_hbm.1, bf16[128,4096]{1,0:T(8,128)(2,1)} %bitcast.11, bf16[1,128]{1,0:T(2,128)(2,1)} %bitcast.14, bf16[4096,256]{1,0:T(8,128)(2,1)} %bitcast.8, bf16[4096,256]{1,0:T(8,128)(2,1)} %bitcast.9, ...), custom_call_target="tpu_custom_call" | custom-call | tf_op jit(solution)/shard_map/merge_moe/pallas_call | solution.py:552
  114.1 1.5 %copy.12 = bf16[256,128]{1,0:T(8,128)(2,1)} copy(bf16[256,128]{1,0:T(8,128)(2,1)} %merge_moe.1) | data formatting | bytes 131072

commit v7 on v6

--- a/solution.py
+++ b/solution.py
@@ -172,12 +172,6 @@
         first, second = hit & (ids[0:1] == x), hit & (ids[1:2] == x)
         sel[x * CAP:(x + 1) * CAP] = (first | second).astype(BF16)
         gsum[x * CAP:(x + 1) * CAP] = jnp.where(first, gates[0], 0.0) + jnp.where(second, gates[1], 0.0)
-    gt = gsum[...].T
-    hi = gt.astype(BF16)
-    g_hi[...] = hi
-    g_lo[...] = (gt - hi.astype(F32)).astype(BF16)
-    acc[...] = jnp.zeros_like(acc)
-    sq[...] = jnp.zeros_like(sq)
 
     def attn_part(k):
         return jnp.dot(heads_v[...], merged[k].reshape(CW, CW), preferred_element_type=F32)
@@ -354,7 +348,13 @@
     drain_a, pend[:] = pend[:-9], pend[-9:]
     for cp in drain_a:
         cp.wait_send()
+    acc[...] = jnp.zeros_like(acc)
+    sq[...] = jnp.zeros_like(sq)
     gate_up(me)
+    gt = gsum[...].T
+    hi = gt.astype(BF16)
+    g_hi[...] = hi
+    g_lo[...] = (gt - hi.astype(F32)).astype(BF16)
     agy_copy(0, other).wait_recv()
     for d in range(2):
         start(ag_copy(d, 2, 0, other))

time: 116 us -> 116 us (level)
  no operation moved by 1% of the time
where the time goes in v7:
time: 116 us
  Pallas kernels  114 us (98%)
  local copies, waits for them, and re-layouts  1.47 us (1%)
    pallas_call x1, Pallas kernels, per_device(): pl.pallas_call(kernel, out_shape=jax.ShapeDtypeStruct((TOK, FW), BF16), i...  114 us

profile of v7, /device:TPU:1, one launch (start us, length us, event | category | flops | bytes accessed | tf_op | source)
XLA Modules:
  0.0 115.6 jit_solution(7014140493327815909)
XLA Ops:
  0.0 114.1 %merge_moe.1 = bf16[256,128]{1,0:T(8,128)(2,1)} custom-call(bf16[256,128]{1,0:T(8,128)(2,1)} %res_hbm.1, bf16[256,128]{1,0:T(8,128)(2,1)} %heads_hbm.1, bf16[128,4096]{1,0:T(8,128)(2,1)} %bitcast.11, bf16[1,128]{1,0:T(2,128)(2,1)} %bitcast.14, bf16[4096,256]{1,0:T(8,128)(2,1)} %bitcast.8, bf16[4096,256]{1,0:T(8,128)(2,1)} %bitcast.9, ...), custom_call_target="tpu_custom_call" | custom-call | tf_op jit(solution)/shard_map/merge_moe/pallas_call | solution.py:552
  114.1 1.5 %copy.12 = bf16[256,128]{1,0:T(8,128)(2,1)} copy(bf16[256,128]{1,0:T(8,128)(2,1)} %merge_moe.1) | data formatting | bytes 131072
